TPU v7x, 256 devices: a whole 4x4x8 slice. The times are simulated.
256 devices in a mesh: dp: 4 (over z_lo), seq: 32 (over x, y, core), tp: 2 (over z_hi).
Axes of the slice: x: 4, y: 4, z: 8 (z_hi: 2, z_lo: 4; z = z_hi * 4 + z_lo), core: 2. Of those that a mesh axis runs over, the one named last changes fastest.
Arguments:
- query: bfloat16 [4, 16384, 512], P('dp', 'seq', 'tp'), may hold values from -6 to 6
- key_in: bfloat16 [4, 16384, 512], P('dp', 'seq', 'tp'), may hold values from -6 to 6
- value: bfloat16 [4, 16384, 512], P('dp', 'seq', 'tp'), may hold values from -6 to 6
- grad_out: bfloat16 [4, 16384, 512], P('dp', 'seq', 'tp'), may hold values from -6 to 6
- filter_taps: float32 [16384, 512], P('seq', 'tp'), may hold values from -1 to 1, as said below
Outputs:
- grad_query: bfloat16 [4, 16384, 512], P('dp', 'seq', 'tp')
- grad_key: bfloat16 [4, 16384, 512], P('dp', 'seq', 'tp')
- grad_value: bfloat16 [4, 16384, 512], P('dp', 'seq', 'tp')
- filter_grad: float32 [16384, 512], P('seq', 'tp')
Inputs may be any that keep to these rules, and one draw needn't show every extreme that they name: `filter_taps`: filter taps of each channel over 16384 positions.
All inputs are finite; a program needn't handle non-finite values.
Results may differ from a plain program's by a relative error of at most 0.0015.
Values sent between devices are 32-bit elements; how exact they have to be, the bound alone decides.
A program may use at most 128 MiB of HBM per device.

v0:
```python
import math

import jax
import jax.numpy as jnp
from jax import lax
from jax.sharding import PartitionSpec as P

highest_mode = lax.Precision.HIGHEST


def angle_pair(index_grid, period_len):
    reduced = index_grid % period_len
    angles = reduced.astype(jnp.float32) * (2.0 * math.pi / period_len)
    return (jnp.cos(angles), jnp.sin(angles))


def make_tables(seq_count, seq_index, cell_count):
    block_len = cell_count // seq_count
    period_len = 2 * seq_count * cell_count
    freq_rows = jnp.arange(2 * seq_count, dtype=jnp.int32)
    coarse_table = angle_pair(
        freq_rows[:, None] * jnp.arange(seq_count, dtype=jnp.int32)[None, :], 2 * seq_count
    )
    cell_index = jnp.arange(cell_count, dtype=jnp.int32)
    fine_table = angle_pair(cell_index[:, None] * cell_index[None, :], cell_count)
    local_cells = seq_index * block_len + jnp.arange(block_len, dtype=jnp.int32)
    twiddle_fwd = angle_pair(freq_rows[:, None] * local_cells[None, :], period_len)
    own_freq = 2 * seq_index + jnp.arange(2, dtype=jnp.int32)
    twiddle_inv = angle_pair(own_freq[:, None] * cell_index[None, :], period_len)
    return (coarse_table, fine_table, twiddle_fwd, twiddle_inv)


def forward_spectrum(signal, tables):
    coarse_table, fine_table, twiddle_fwd, twiddle_inv = tables
    seq_count = lax.axis_size("seq")
    cell_count, chan_count = signal.shape
    block_len = cell_count // seq_count
    moved = lax.all_to_all(signal, "seq", split_axis=0, concat_axis=0, tiled=True).reshape(
        seq_count, block_len, chan_count
    )
    real_a = jnp.einsum("kp,pjc->kjc", coarse_table[0], moved, precision=highest_mode)
    imag_a = -jnp.einsum("kp,pjc->kjc", coarse_table[1], moved, precision=highest_mode)
    turn_cos = twiddle_fwd[0][:, :, None]
    turn_sin = twiddle_fwd[1][:, :, None]
    real_b = real_a * turn_cos + imag_a * turn_sin
    imag_b = imag_a * turn_cos - real_a * turn_sin
    real_b, imag_b = (
        lax.all_to_all(real_b, "seq", split_axis=0, concat_axis=1, tiled=True),
        lax.all_to_all(imag_b, "seq", split_axis=0, concat_axis=1, tiled=True),
    )
    fine_cos, fine_sin = fine_table
    spec_real = jnp.einsum("kj,ajc->akc", fine_cos, real_b, precision=highest_mode) + jnp.einsum(
        "kj,ajc->akc", fine_sin, imag_b, precision=highest_mode
    )
    spec_imag = jnp.einsum("kj,ajc->akc", fine_cos, imag_b, precision=highest_mode) - jnp.einsum(
        "kj,ajc->akc", fine_sin, real_b, precision=highest_mode
    )
    return (spec_real, spec_imag)


def inverse_signal(spec_real, spec_imag, tables):
    coarse_table, fine_table, twiddle_fwd, twiddle_inv = tables
    seq_count = lax.axis_size("seq")
    cell_count = spec_real.shape[1]
    chan_count = spec_real.shape[2]
    period_len = 2 * seq_count * cell_count
    fine_cos, fine_sin = fine_table
    back_real = jnp.einsum("kj,akc->ajc", fine_cos, spec_real, precision=highest_mode) - jnp.einsum(
        "kj,akc->ajc", fine_sin, spec_imag, precision=highest_mode
    )
    back_imag = jnp.einsum("kj,akc->ajc", fine_cos, spec_imag, precision=highest_mode) + jnp.einsum(
        "kj,akc->ajc", fine_sin, spec_real, precision=highest_mode
    )
    turn_cos = twiddle_inv[0][:, :, None]
    turn_sin = twiddle_inv[1][:, :, None]
    turned_real = back_real * turn_cos - back_imag * turn_sin
    turned_imag = back_imag * turn_cos + back_real * turn_sin
    turned_real, turned_imag = (
        lax.all_to_all(turned_real, "seq", split_axis=1, concat_axis=0, tiled=True),
        lax.all_to_all(turned_imag, "seq", split_axis=1, concat_axis=0, tiled=True),
    )
    values = jnp.einsum(
        "kp,kjc->pjc", coarse_table[0], turned_real, precision=highest_mode
    ) - jnp.einsum("kp,kjc->pjc", coarse_table[1], turned_imag, precision=highest_mode)
    values = values * (1.0 / period_len)
    values = lax.all_to_all(values, "seq", split_axis=0, concat_axis=1, tiled=True)
    return values.reshape(cell_count, chan_count)


def shards(query, key_in, value, grad_out, filter_taps):
    seq_count = lax.axis_size("seq")
    seq_index = lax.axis_index("seq")
    data_count = lax.axis_size("dp")
    cell_count = query.shape[1]
    query_f = query[0].astype(jnp.float32)
    key_f = key_in[0].astype(jnp.float32)
    value_f = value[0].astype(jnp.float32)
    grad_f = grad_out[0].astype(jnp.float32)
    gated = key_f * value_f
    dgate = grad_f * query_f
    scale_factor = 1.0 / math.sqrt(data_count * cell_count * seq_count)
    tables = make_tables(seq_count, seq_index, cell_count)
    gate_real, gate_imag = forward_spectrum(gated, tables)
    taps_real, taps_imag = forward_spectrum(filter_taps, tables)
    dgate_real, dgate_imag = forward_spectrum(dgate, tables)
    conv_real = taps_real * gate_real - taps_imag * gate_imag
    conv_imag = taps_real * gate_imag + taps_imag * gate_real
    adj_real = taps_real * dgate_real + taps_imag * dgate_imag
    adj_imag = taps_real * dgate_imag - taps_imag * dgate_real
    corr_real = (gate_real * dgate_real + gate_imag * dgate_imag) * scale_factor
    corr_imag = (gate_real * dgate_imag - gate_imag * dgate_real) * scale_factor
    convolved = inverse_signal(conv_real, conv_imag, tables)
    adjoint = inverse_signal(adj_real, adj_imag, tables)
    filter_part = inverse_signal(corr_real, corr_imag, tables)
    filter_grad = lax.psum(filter_part, "dp")
    grad_query = (grad_f * convolved).astype(jnp.bfloat16)[None]
    grad_key = (adjoint * value_f).astype(jnp.bfloat16)[None]
    grad_value = (adjoint * key_f).astype(jnp.bfloat16)[None]
    return (grad_query, grad_key, grad_value, filter_grad)


def solution(mesh):
    in_specs = (
        P("dp", "seq", "tp"),
        P("dp", "seq", "tp"),
        P("dp", "seq", "tp"),
        P("dp", "seq", "tp"),
        P("seq", "tp"),
    )
    out_specs = (P("dp", "seq", "tp"), P("dp", "seq", "tp"), P("dp", "seq", "tp"), P("seq", "tp"))
    return jax.shard_map(shards, mesh=mesh, in_specs=in_specs, out_specs=out_specs, check_vma=False)
```

profile of v0, /device:TPU:1, one launch (start us, length us, event | category | flops | bytes accessed | tf_op | source)
XLA Modules:
  0.0 594.2 jit_solution(9051378448649368390)
XLA Ops:
  9.1 8.7 %all-to-all-start.3 = ((f32[32,16,256]{2,1,0:T(8,128)}), f32[32,16,256]{2,1,0:T(8,128)S(1)}, u32[]{:S(2)}, u32[]{:S(2)}) async-start(f32[32,16,256]{2,1,0:T(8,128)} %bitcast.11), calls=%async_computation.3 | async-start | bytes 1048576 | tf_op jit(solution)/shard_map/all_to_all | solution.py:38
  18.8 10.6 %all-to-all-done.3 = f32[32,16,256]{2,1,0:T(8,128)S(1)} async-done(((f32[32,16,256]{2,1,0:T(8,128)}), f32[32,16,256]{2,1,0:T(8,128)S(1)}, u32[]{:S(2)}, u32[]{:S(2)}) %all-to-all-start.3) | async-done | bytes 524320 | tf_op jit(solution)/shard_map/all_to_all | solution.py:38
  29.4 3.7 all-to-all-start
  37.7 7.0 %all-to-all-done = f32[32,16,256]{2,1,0:T(8,128)S(1)} async-done(((f32[32,16,256]{2,1,0:T(8,128)}), f32[32,16,256]{2,1,0:T(8,128)S(1)}, u32[]{:S(2)}, u32[]{:S(2)}) %all-to-all-start) | async-done | bytes 524320 | tf_op jit(solution)/shard_map/all_to_all | solution.py:38
  44.7 3.7 all-to-all-start.9
  48.4 2.3 convolution_negate_fusion.2
  50.7 2.3 fusion.93
  53.0 6.9 %all-to-all-done.9 = f32[32,16,256]{2,1,0:T(8,128)S(1)} async-done(((f32[32,16,256]{2,1,0:T(8,128)}), f32[32,16,256]{2,1,0:T(8,128)S(1)}, u32[]{:S(2)}, u32[]{:S(2)}) %all-to-all-start.9) | async-done | bytes 524320 | tf_op jit(solution)/shard_map/all_to_all | solution.py:38
  61.3 4.5 multiply_subtract_fusion.1
  67.3 4.6 all-to-all-start.1
  73.5 15.0 %all-to-all-done.1 = f32[64,16,256]{2,1,0:T(8,128)} async-done(((f32[64,16,256]{2,1,0:T(8,128)}), f32[64,16,256]{2,1,0:T(8,128)}, u32[]{:S(2)}, u32[]{:S(2)}) %all-to-all-start.1) | async-done | bytes 1048608 | tf_op jit(solution)/shard_map/all_to_all | solution.py:48
  88.5 5.0 all-to-all-start.2
  95.2 15.3 %all-to-all-done.2 = f32[64,16,256]{2,1,0:T(8,128)} async-done(((f32[64,16,256]{2,1,0:T(8,128)}), f32[64,16,256]{2,1,0:T(8,128)}, u32[]{:S(2)}, u32[]{:S(2)}) %all-to-all-start.2) | async-done | bytes 1048608 | tf_op jit(solution)/shard_map/all_to_all | solution.py:49
  110.5 4.5 all-to-all-start.10
  116.6 15.4 %all-to-all-done.10 = f32[64,16,256]{2,1,0:T(8,128)} async-done(((f32[64,16,256]{2,1,0:T(8,128)}), f32[64,16,256]{2,1,0:T(8,128)}, u32[]{:S(2)}, u32[]{:S(2)}) %all-to-all-start.10) | async-done | bytes 1048608 | tf_op jit(solution)/shard_map/all_to_all | solution.py:48
  132.0 3.9 all-to-all-start.11
  137.5 15.3 %all-to-all-done.11 = f32[64,16,256]{2,1,0:T(8,128)S(1)} async-done(((f32[64,16,256]{2,1,0:T(8,128)}), f32[64,16,256]{2,1,0:T(8,128)S(1)}, u32[]{:S(2)}, u32[]{:S(2)}) %all-to-all-start.11) | async-done | bytes 1048608 | tf_op jit(solution)/shard_map/all_to_all | solution.py:49
  152.8 4.0 all-to-all-start.4
  164.4 7.9 %fusion.52 = f32[2,256,512]{2,1,0:T(8,128)} fusion(f32[2,512,256]{2,1,0:T(8,128)S(1)} %bitcast.224), kind=kOutput, calls=%fused_computation.73 | convolution fusion | flops 1614282752 | bytes 2097152 | tf_op jit(solution)/shard_map/kj,ajc->akc/dot_general | solution.py:52
  172.3 8.0 %fusion.48 = f32[2,256,512]{2,1,0:T(8,128)} fusion(f32[2,512,256]{2,1,0:T(8,128)S(1)} %bitcast.228), kind=kOutput, calls=%fused_computation.69 | convolution fusion | flops 1614282752 | bytes 2097152 | tf_op jit(solution)/shard_map/kj,ajc->akc/dot_general | solution.py:55
  180.3 8.1 %fusion.42 = f32[2,256,512]{2,1,0:T(8,128)} fusion(f32[2,512,256]{2,1,0:T(8,128)S(1)} %bitcast.222), kind=kOutput, calls=%fused_computation.63 | convolution fusion | flops 1614282752 | bytes 2097152 | tf_op jit(solution)/shard_map/kj,ajc->akc/dot_general | solution.py:52
  188.4 7.4 %all-to-all-start.5 = ((f32[64,16,256]{2,1,0:T(8,128)}), f32[64,16,256]{2,1,0:T(8,128)S(1)}, u32[]{:S(2)}, u32[]{:S(2)}) async-start(f32[64,16,256]{2,1,0:T(8,128)} %copy.115), calls=%async_computation.5 | async-start | bytes 2097152 | tf_op jit(solution)/shard_map/all_to_all | solution.py:49
  195.9 8.0 %fusion.50 = f32[2,256,512]{2,1,0:T(8,128)} fusion(f32[2,512,256]{2,1,0:T(8,128)S(1)} %bitcast.218), kind=kOutput, calls=%fused_computation.71 | convolution fusion | flops 1614282752 | bytes 2097152 | tf_op jit(solution)/shard_map/kj,ajc->akc/dot_general | solution.py:52
  203.9 8.0 %fusion.40 = f32[2,256,512]{2,1,0:T(8,128)} fusion(f32[2,512,256]{2,1,0:T(8,128)S(1)} %bitcast.226), kind=kOutput, calls=%fused_computation.61 | convolution fusion | flops 1614282752 | bytes 2097152 | tf_op jit(solution)/shard_map/kj,ajc->akc/dot_general | solution.py:55
  211.9 8.0 %convolution_add_fusion.5 = f32[2,256,512]{2,1,0:T(8,128)} fusion(f32[2,256,512]{2,1,0:T(8,128)S(1)} %copy-done.24, f32[2,512,256]{2,1,0:T(8,128)S(1)} %bitcast.229), kind=kOutput, calls=%fused_computation.17 | convolution fusion | flops 1614544896 | bytes 3145728 | tf_op jit(solution)/shard_map/kj,ajc->akc/dot_general | solution.py:52
  220.0 8.4 %convolution_subtract_fusion.5 = f32[2,256,512]{2,1,0:T(8,128)} fusion(f32[2,256,512]{2,1,0:T(8,128)S(1)} %copy-done.22, f32[2,512,256]{2,1,0:T(8,128)S(1)} %bitcast.225), kind=kOutput, calls=%fused_computation.15 | convolution fusion | flops 1614544896 | bytes 3145728 | tf_op jit(solution)/shard_map/kj,ajc->akc/dot_general | solution.py:55
  228.4 8.0 %convolution_add_fusion.2 = f32[2,256,512]{2,1,0:T(8,128)} fusion(f32[2,256,512]{2,1,0:T(8,128)S(1)} %copy-done.20, f32[2,512,256]{2,1,0:T(8,128)S(1)} %bitcast.227), kind=kOutput, calls=%fused_computation.11 | convolution fusion | flops 1614544896 | bytes 3145728 | tf_op jit(solution)/shard_map/kj,ajc->akc/dot_general | solution.py:52
  236.4 7.5 %fusion.46 = f32[2,256,512]{2,1,0:T(8,128)S(1)} fusion(f32[2,512,256]{2,1,0:T(8,128)S(1)} %bitcast.230), kind=kOutput, calls=%fused_computation.67 | convolution fusion | flops 1614282752 | bytes 2097152 | tf_op jit(solution)/shard_map/kj,ajc->akc/dot_general | solution.py:55
  244.0 7.7 %convolution_add_fusion.4 = f32[2,256,512]{2,1,0:T(8,128)S(1)} fusion(f32[2,256,512]{2,1,0:T(8,128)S(1)} %copy-done.23, f32[2,512,256]{2,1,0:T(8,128)S(1)} %bitcast.231), kind=kOutput, calls=%fused_computation.16 | convolution fusion | flops 1614544896 | bytes 3145728 | tf_op jit(solution)/shard_map/kj,ajc->akc/dot_general | solution.py:52
  251.8 7.6 %convolution_subtract_fusion.2 = f32[2,256,512]{2,1,0:T(8,128)S(1)} fusion(f32[2,256,512]{2,1,0:T(8,128)S(1)} %copy-done.21, f32[2,512,256]{2,1,0:T(8,128)S(1)} %bitcast.223), kind=kOutput, calls=%fused_computation.10 | convolution fusion | flops 1614544896 | bytes 3145728 | tf_op jit(solution)/shard_map/kj,ajc->akc/dot_general | solution.py:55
  259.4 8.1 %add_multiply_fusion = (f32[2,256,512]{2,1,0:T(8,128)S(1)}, f32[2,256,512]{2,1,0:T(8,128)S(1)}, f32[2,256,512]{2,1,0:T(8,128)S(1)}, f32[2,256,512]{2,1,0:T(8,128...) fusion(f32[2,256,512]{2,1,0:T(8,128)S(1)} %convolution_subtract_fusion.2, ...), kind=kOutput, calls=%fused_computation.78 | convolution fusion | flops 1619787776 | bytes 13631488 | tf_op jit(solution)/shard_map/kj,ajc->akc/dot_general | solution.py:55
  267.5 6.5 %fusion.16 = f32[2,256,512]{2,1,0:T(8,128)S(1)} fusion(f32[2,256,512]{2,1,0:T(8,128)S(1)} %get-tuple-element.23), kind=kOutput, calls=%fused_computation.37 | convolution fusion | flops 1614282752 | bytes 2097152 | tf_op jit(solution)/shard_map/kj,akc->ajc/dot_general | solution.py:68
  274.0 6.3 %fusion.12 = f32[2,256,512]{2,1,0:T(8,128)S(1)} fusion(f32[2,256,512]{2,1,0:T(8,128)S(1)} %get-tuple-element.22), kind=kOutput, calls=%fused_computation.33 | convolution fusion | flops 1614282752 | bytes 2097152 | tf_op jit(solution)/shard_map/kj,akc->ajc/dot_general | solution.py:71
  280.4 6.3 %convolution_subtract_fusion.1 = f32[2,256,512]{2,1,0:T(8,128)S(1)} fusion(f32[2,256,512]{2,1,0:T(8,128)S(1)} %fusion.16, f32[2,256,512]{2,1,0:T(8,128)S(1)} %get-tuple-element.22), kind=kOutput, calls=%fused_computation.9 | convolution fusion | flops 1614544896 | bytes 3145728 | tf_op jit(solution)/shard_map/kj,akc->ajc/dot_general | solution.py:68
  286.7 6.7 %convolution_add_fusion.1 = f32[2,256,512]{2,1,0:T(8,128)S(1)} fusion(f32[2,256,512]{2,1,0:T(8,128)S(1)} %fusion.12, f32[2,256,512]{2,1,0:T(8,128)S(1)} %get-tuple-element.23), kind=kOutput, calls=%fused_computation.8 | convolution fusion | flops 1614544896 | bytes 3145728 | tf_op jit(solution)/shard_map/kj,akc->ajc/dot_general | solution.py:71
  293.4 6.3 %fusion.18 = f32[2,256,512]{2,1,0:T(8,128)S(1)} fusion(f32[2,256,512]{2,1,0:T(8,128)S(1)} %get-tuple-element.24), kind=kOutput, calls=%fused_computation.39 | convolution fusion | flops 1614282752 | bytes 2097152 | tf_op jit(solution)/shard_map/kj,akc->ajc/dot_general | solution.py:71
  299.7 6.3 %fusion.22 = f32[2,256,512]{2,1,0:T(8,128)S(1)} fusion(f32[2,256,512]{2,1,0:T(8,128)S(1)} %get-tuple-element.25), kind=kOutput, calls=%fused_computation.43 | convolution fusion | flops 1614282752 | bytes 2097152 | tf_op jit(solution)/shard_map/kj,akc->ajc/dot_general | solution.py:68
  306.1 6.5 %convolution_add_fusion.3 = f32[2,256,512]{2,1,0:T(8,128)S(1)} fusion(f32[2,256,512]{2,1,0:T(8,128)S(1)} %fusion.18, f32[2,256,512]{2,1,0:T(8,128)S(1)} %get-tuple-element.25), kind=kOutput, calls=%fused_computation.12 | convolution fusion | flops 1614544896 | bytes 3145728 | tf_op jit(solution)/shard_map/kj,akc->ajc/dot_general | solution.py:71
  312.6 6.3 %fusion.6 = f32[2,256,512]{2,1,0:T(8,128)S(1)} fusion(f32[2,256,512]{2,1,0:T(8,128)S(1)} %get-tuple-element.5), kind=kOutput, calls=%fused_computation.27 | convolution fusion | flops 1614282752 | bytes 2097152 | tf_op jit(solution)/shard_map/kj,akc->ajc/dot_general | solution.py:71
  318.9 6.3 %fusion.10 = f32[2,256,512]{2,1,0:T(8,128)S(1)} fusion(f32[2,256,512]{2,1,0:T(8,128)S(1)} %get-tuple-element.4), kind=kOutput, calls=%fused_computation.31 | convolution fusion | flops 1614282752 | bytes 2097152 | tf_op jit(solution)/shard_map/kj,akc->ajc/dot_general | solution.py:68
  325.2 6.5 %convolution_add_fusion = f32[2,256,512]{2,1,0:T(8,128)S(1)} fusion(f32[2,256,512]{2,1,0:T(8,128)S(1)} %fusion.6, f32[2,256,512]{2,1,0:T(8,128)S(1)} %get-tuple-element.4), kind=kOutput, calls=%fused_computation.6 | convolution fusion | flops 1614544896 | bytes 3145728 | tf_op jit(solution)/shard_map/kj,akc->ajc/dot_general | solution.py:71
  331.7 6.3 %convolution_subtract_fusion = f32[2,256,512]{2,1,0:T(8,128)S(1)} fusion(f32[2,256,512]{2,1,0:T(8,128)S(1)} %fusion.10, f32[2,256,512]{2,1,0:T(8,128)S(1)} %get-tuple-element.5), kind=kOutput, calls=%fused_computation.7 | convolution fusion | flops 1614544896 | bytes 3145728 | tf_op jit(solution)/shard_map/kj,akc->ajc/dot_general | solution.py:68
  338.1 7.5 %add_bitcast_fusion = (f32[2,512,256]{1,2,0:T(8,128)}, f32[2,512,256]{1,2,0:T(8,128)}, f32[2,512,256]{1,2,0:T(8,128)S(1)}, f32[2,512,256]{1,2,0:T(8,128)S(1)}, f...) fusion(f32[2,256,512]{2,1,0:T(8,128)S(1)} %convolution_subtract_fusion, f32[2,256,512]{2,1,0:T(8,128)S(1)} %convolution_add_fusion, ...), kind=kOutput, calls=%fused_computation.75 | convolution fusion | flops 1619263488 | bytes 13639680 | tf_op jit(solution)/shard_map/kj,akc->ajc/dot_general | solution.py:68
  347.9 7.4 %all-to-all-start.15 = ((f32[2,512,256]{2,0,1:T(2,128)}), f32[2,512,256]{2,0,1:T(2,128)}, u32[]{:S(2)}, u32[]{:S(2)}) async-start(f32[2,512,256]{2,0,1:T(2,128)} %copy.146), calls=%async_computation.15 | async-start | bytes 2097152 | tf_op jit(solution)/shard_map/all_to_all | solution.py:79
  357.6 14.7 %all-to-all-done.15 = f32[2,512,256]{2,0,1:T(2,128)} async-done(((f32[2,512,256]{2,0,1:T(2,128)}), f32[2,512,256]{2,0,1:T(2,128)}, u32[]{:S(2)}, u32[]{:S(2)}) %all-to-all-start.15) | async-done | bytes 1048608 | tf_op jit(solution)/shard_map/all_to_all | solution.py:79
  372.3 4.4 all-to-all-start.16
  379.0 14.7 %all-to-all-done.16 = f32[2,512,256]{2,0,1:T(2,128)} async-done(((f32[2,512,256]{2,0,1:T(2,128)}), f32[2,512,256]{2,0,1:T(2,128)}, u32[]{:S(2)}, u32[]{:S(2)}) %all-to-all-start.16) | async-done | bytes 1048608 | tf_op jit(solution)/shard_map/all_to_all | solution.py:80
  393.7 4.4 all-to-all-start.12
  399.5 15.7 %all-to-all-done.12 = f32[2,512,256]{2,0,1:T(2,128)} async-done(((f32[2,512,256]{2,0,1:T(2,128)}), f32[2,512,256]{2,0,1:T(2,128)}, u32[]{:S(2)}, u32[]{:S(2)}) %all-to-all-start.12) | async-done | bytes 1048608 | tf_op jit(solution)/shard_map/all_to_all | solution.py:79
  415.2 4.3 all-to-all-start.13
  420.8 15.6 %all-to-all-done.13 = f32[2,512,256]{2,0,1:T(2,128)S(1)} async-done(((f32[2,512,256]{2,0,1:T(2,128)}), f32[2,512,256]{2,0,1:T(2,128)S(1)}, u32[]{:S(2)}, u32[]{:S(2)}) %all-to-all-start.13) | async-done | bytes 1048608 | tf_op jit(solution)/shard_map/all_to_all | solution.py:80
  436.4 4.0 all-to-all-start.6
  441.7 15.6 %all-to-all-done.6 = f32[2,512,256]{2,0,1:T(2,128)S(1)} async-done(((f32[2,512,256]{2,0,1:T(2,128)}), f32[2,512,256]{2,0,1:T(2,128)S(1)}, u32[]{:S(2)}, u32[]{:S(2)}) %all-to-all-start.6) | async-done | bytes 1048608 | tf_op jit(solution)/shard_map/all_to_all | solution.py:79
  457.3 4.0 all-to-all-start.7
  464.4 2.9 all_to_all.240
  470.4 2.9 all_to_all.244
  480.3 2.9 all_to_all.231
  490.9 7.6 %all-to-all-start.17 = ((f32[32,16,256]{2,1,0:T(8,128)}), f32[32,16,256]{2,1,0:T(8,128)}, u32[]{:S(2)}, u32[]{:S(2)}) async-start(f32[32,16,256]{2,1,0:T(8,128)} %copy.152), calls=%async_computation.17 | async-start | bytes 1048576 | tf_op jit(solution)/shard_map/all_to_all | solution.py:86
  504.9 5.3 all-to-all-done.17
  510.2 3.7 all-to-all-start.8
  516.4 9.1 %all-to-all-done.8 = f32[32,16,256]{2,1,0:T(8,128)S(1)} async-done(((f32[32,16,256]{2,1,0:T(8,128)}), f32[32,16,256]{2,1,0:T(8,128)S(1)}, u32[]{:S(2)}, u32[]{:S(2)}) %all-to-all-start.8) | async-done | bytes 524320 | tf_op jit(solution)/shard_map/all_to_all | solution.py:86
  525.4 3.7 all-to-all-start.14
  530.6 10.1 %all-to-all-done.14 = f32[32,16,256]{2,1,0:T(8,128)S(1)} async-done(((f32[32,16,256]{2,1,0:T(8,128)}), f32[32,16,256]{2,1,0:T(8,128)S(1)}, u32[]{:S(2)}, u32[]{:S(2)}) %all-to-all-start.14) | async-done | bytes 524320 | tf_op jit(solution)/shard_map/all_to_all | solution.py:86
  541.6 43.8 %all-reduce.2.cloned.1.call-done = f32[512,256]{1,0:T(8,128)} async-done(((f32[512,256]{1,0:T(8,128)}), f32[512,256]{1,0:T(8,128)}) %all-reduce.2.cloned.1.call-update) | async-done | bytes 524304 | tf_op jit(solution)/shard_map/psum | solution.py:115
  (109 shorter events, 69.2 us)
Async XLA Ops:
  9.1 8.9 %copy-start.13 = (bf16[1,512,256]{2,1,0:T(8,128)(2,1)S(1)}, bf16[1,512,256]{2,1,0:T(8,128)(2,1)}, u32[]{:S(2)}) copy-start(bf16[1,512,256]{2,1,0:T(8,128)(2,1)} %param.8) | copy-start | bytes 786436
  9.1 8.9 %copy-start.19 = (bf16[1,512,256]{2,1,0:T(8,128)(2,1)S(1)}, bf16[1,512,256]{2,1,0:T(8,128)(2,1)}, u32[]{:S(2)}) copy-start(bf16[1,512,256]{2,1,0:T(8,128)(2,1)} %param.5) | copy-start | bytes 786436
  9.1 20.4 %all-to-all-start.3 = ((f32[32,16,256]{2,1,0:T(8,128)}), f32[32,16,256]{2,1,0:T(8,128)S(1)}, u32[]{:S(2)}, u32[]{:S(2)}) async-start(f32[32,16,256]{2,1,0:T(8,128)} %bitcast.11), calls=%async_computation.3 | async-start | bytes 1048576 | tf_op jit(solution)/shard_map/all_to_all | solution.py:38
  29.4 15.3 %all-to-all-start = ((f32[32,16,256]{2,1,0:T(8,128)}), f32[32,16,256]{2,1,0:T(8,128)S(1)}, u32[]{:S(2)}, u32[]{:S(2)}) async-start(f32[32,16,256]{2,1,0:T(8,128)} %bitcast.1), calls=%async_computation | async-start | bytes 1048576 | tf_op jit(solution)/shard_map/all_to_all | solution.py:38
  44.7 15.3 %all-to-all-start.9 = ((f32[32,16,256]{2,1,0:T(8,128)}), f32[32,16,256]{2,1,0:T(8,128)S(1)}, u32[]{:S(2)}, u32[]{:S(2)}) async-start(f32[32,16,256]{2,1,0:T(8,128)} %bitcast.27), calls=%async_computation.9 | async-start | bytes 1048576 | tf_op jit(solution)/shard_map/all_to_all | solution.py:38
  59.9 1.3 copy-start.2
  67.3 4.6 copy-start.3
  67.3 21.2 %all-to-all-start.1 = ((f32[64,16,256]{2,1,0:T(8,128)}), f32[64,16,256]{2,1,0:T(8,128)}, u32[]{:S(2)}, u32[]{:S(2)}) async-start(f32[64,16,256]{2,1,0:T(8,128)} %copy.104), calls=%async_computation.1 | async-start | bytes 2097152 | tf_op jit(solution)/shard_map/all_to_all | solution.py:48
  73.5 20.1 %copy-start.1 = (f32[64,16,256]{2,0,1:T(8,128)S(1)}, f32[64,16,256]{2,0,1:T(8,128)}, u32[]{:S(2)}) copy-start(f32[64,16,256]{2,0,1:T(8,128)} %get-tuple-element.11) | copy-start | bytes 3145732
  88.5 21.9 %all-to-all-start.2 = ((f32[64,16,256]{2,1,0:T(8,128)}), f32[64,16,256]{2,1,0:T(8,128)}, u32[]{:S(2)}, u32[]{:S(2)}) async-start(f32[64,16,256]{2,1,0:T(8,128)} %copy.107), calls=%async_computation.2 | async-start | bytes 2097152 | tf_op jit(solution)/shard_map/all_to_all | solution.py:49
  95.2 19.7 %copy-start = (f32[64,16,256]{2,0,1:T(8,128)S(1)}, f32[64,16,256]{2,0,1:T(8,128)}, u32[]{:S(2)}) copy-start(f32[64,16,256]{2,0,1:T(8,128)} %get-tuple-element.10) | copy-start | bytes 3145732
  110.5 21.5 %all-to-all-start.10 = ((f32[64,16,256]{2,1,0:T(8,128)}), f32[64,16,256]{2,1,0:T(8,128)}, u32[]{:S(2)}, u32[]{:S(2)}) async-start(f32[64,16,256]{2,1,0:T(8,128)} %copy.131), calls=%async_computation.10 | async-start | bytes 2097152 | tf_op jit(solution)/shard_map/all_to_all | solution.py:48
  132.0 20.9 %all-to-all-start.11 = ((f32[64,16,256]{2,1,0:T(8,128)}), f32[64,16,256]{2,1,0:T(8,128)S(1)}, u32[]{:S(2)}, u32[]{:S(2)}) async-start(f32[64,16,256]{2,1,0:T(8,128)} %copy.134), calls=%async_computation.11 | async-start | bytes 2097152 | tf_op jit(solution)/shard_map/all_to_all | solution.py:49
  152.8 35.6 %all-to-all-start.4 = ((f32[64,16,256]{2,1,0:T(8,128)}), f32[64,16,256]{2,1,0:T(8,128)S(1)}, u32[]{:S(2)}, u32[]{:S(2)}) async-start(f32[64,16,256]{2,1,0:T(8,128)} %copy.112), calls=%async_computation.4 | async-start | bytes 2097152 | tf_op jit(solution)/shard_map/all_to_all | solution.py:48
  159.9 4.5 copy-start.8
  161.6 10.8 %copy-start.11 = (f32[2,32,16,256]{3,2,1,0:T(8,128)}, f32[2,32,16,256]{3,2,1,0:T(8,128)S(1)}, u32[]{:S(2)}) copy-start(f32[2,32,16,256]{3,2,1,0:T(8,128)S(1)} %copy.108) | copy-start | bytes 3145732
  163.3 17.1 %copy-start.6 = (f32[2,32,16,256]{3,2,1,0:T(8,128)}, f32[2,32,16,256]{3,2,1,0:T(8,128)S(1)}, u32[]{:S(2)}) copy-start(f32[2,32,16,256]{3,2,1,0:T(8,128)S(1)} %copy.132) | copy-start | bytes 3145732
  188.4 47.9 %all-to-all-start.5 = ((f32[64,16,256]{2,1,0:T(8,128)}), f32[64,16,256]{2,1,0:T(8,128)S(1)}, u32[]{:S(2)}, u32[]{:S(2)}) async-start(f32[64,16,256]{2,1,0:T(8,128)} %copy.115), calls=%async_computation.5 | async-start | bytes 2097152 | tf_op jit(solution)/shard_map/all_to_all | solution.py:49
  195.9 8.0 %copy-start.10 = (f32[2,32,16,256]{3,2,1,0:T(8,128)S(1)}, f32[2,32,16,256]{3,2,1,0:T(8,128)}, u32[]{:S(2)}) copy-start(f32[2,32,16,256]{3,2,1,0:T(8,128)} %copy.135) | copy-start | bytes 3145732
  203.9 8.0 %copy-start.12 = (f32[2,32,16,256]{3,2,1,0:T(8,128)S(1)}, f32[2,32,16,256]{3,2,1,0:T(8,128)}, u32[]{:S(2)}) copy-start(f32[2,32,16,256]{3,2,1,0:T(8,128)} %copy-done.11) | copy-start | bytes 3145732
  203.9 8.0 %copy-start.24 = (f32[2,256,512]{2,1,0:T(8,128)S(1)}, f32[2,256,512]{2,1,0:T(8,128)}, u32[]{:S(2)}) copy-start(f32[2,256,512]{2,1,0:T(8,128)} %fusion.52) | copy-start | bytes 3145732
  211.9 8.0 %copy-start.9 = (f32[2,32,16,256]{3,2,1,0:T(8,128)S(1)}, f32[2,32,16,256]{3,2,1,0:T(8,128)}, u32[]{:S(2)}) copy-start(f32[2,32,16,256]{3,2,1,0:T(8,128)} %copy-done.8) | copy-start | bytes 3145732
  211.9 8.0 %copy-start.22 = (f32[2,256,512]{2,1,0:T(8,128)S(1)}, f32[2,256,512]{2,1,0:T(8,128)}, u32[]{:S(2)}) copy-start(f32[2,256,512]{2,1,0:T(8,128)} %fusion.48) | copy-start | bytes 3145732
  220.0 8.4 %copy-start.20 = (f32[2,256,512]{2,1,0:T(8,128)S(1)}, f32[2,256,512]{2,1,0:T(8,128)}, u32[]{:S(2)}) copy-start(f32[2,256,512]{2,1,0:T(8,128)} %fusion.42) | copy-start | bytes 3145732
  236.4 7.5 %copy-start.23 = (f32[2,256,512]{2,1,0:T(8,128)S(1)}, f32[2,256,512]{2,1,0:T(8,128)}, u32[]{:S(2)}) copy-start(f32[2,256,512]{2,1,0:T(8,128)} %fusion.50) | copy-start | bytes 3145732
  244.0 7.8 %copy-start.7 = (f32[2,32,16,256]{3,2,1,0:T(8,128)S(1)}, f32[2,32,16,256]{3,2,1,0:T(8,128)}, u32[]{:S(2)}) copy-start(f32[2,32,16,256]{3,2,1,0:T(8,128)} %copy-done.6) | copy-start | bytes 3145732
  244.0 7.8 %copy-start.21 = (f32[2,256,512]{2,1,0:T(8,128)S(1)}, f32[2,256,512]{2,1,0:T(8,128)}, u32[]{:S(2)}) copy-start(f32[2,256,512]{2,1,0:T(8,128)} %fusion.40) | copy-start | bytes 3145732
  251.8 7.6 %copy-start.16 = (f32[2,256,512]{2,1,0:T(8,128)S(1)}, f32[2,256,512]{2,1,0:T(8,128)}, u32[]{:S(2)}) copy-start(f32[2,256,512]{2,1,0:T(8,128)} %convolution_add_fusion.5) | copy-start | bytes 3145732
  251.8 7.6 %copy-start.17 = (f32[2,256,512]{2,1,0:T(8,128)S(1)}, f32[2,256,512]{2,1,0:T(8,128)}, u32[]{:S(2)}) copy-start(f32[2,256,512]{2,1,0:T(8,128)} %convolution_subtract_fusion.5) | copy-start | bytes 3145732
  251.8 7.6 %copy-start.18 = (f32[2,256,512]{2,1,0:T(8,128)S(1)}, f32[2,256,512]{2,1,0:T(8,128)}, u32[]{:S(2)}) copy-start(f32[2,256,512]{2,1,0:T(8,128)} %convolution_add_fusion.2) | copy-start | bytes 3145732
  347.9 24.4 %all-to-all-start.15 = ((f32[2,512,256]{2,0,1:T(2,128)}), f32[2,512,256]{2,0,1:T(2,128)}, u32[]{:S(2)}, u32[]{:S(2)}) async-start(f32[2,512,256]{2,0,1:T(2,128)} %copy.146), calls=%async_computation.15 | async-start | bytes 2097152 | tf_op jit(solution)/shard_map/all_to_all | solution.py:79
  372.3 21.4 %all-to-all-start.16 = ((f32[2,512,256]{2,0,1:T(2,128)}), f32[2,512,256]{2,0,1:T(2,128)}, u32[]{:S(2)}, u32[]{:S(2)}) async-start(f32[2,512,256]{2,0,1:T(2,128)} %copy.149), calls=%async_computation.16 | async-start | bytes 2097152 | tf_op jit(solution)/shard_map/all_to_all | solution.py:80
  393.7 21.4 %all-to-all-start.12 = ((f32[2,512,256]{2,0,1:T(2,128)}), f32[2,512,256]{2,0,1:T(2,128)}, u32[]{:S(2)}, u32[]{:S(2)}) async-start(f32[2,512,256]{2,0,1:T(2,128)} %copy.139), calls=%async_computation.12 | async-start | bytes 2097152 | tf_op jit(solution)/shard_map/all_to_all | solution.py:79
  415.2 21.3 %all-to-all-start.13 = ((f32[2,512,256]{2,0,1:T(2,128)}), f32[2,512,256]{2,0,1:T(2,128)S(1)}, u32[]{:S(2)}, u32[]{:S(2)}) async-start(f32[2,512,256]{2,0,1:T(2,128)} %copy.142), calls=%async_computation.13 | async-start | bytes 2097152 | tf_op jit(solution)/shard_map/all_to_all | solution.py:80
  436.4 20.9 %all-to-all-start.6 = ((f32[2,512,256]{2,0,1:T(2,128)}), f32[2,512,256]{2,0,1:T(2,128)S(1)}, u32[]{:S(2)}, u32[]{:S(2)}) async-start(f32[2,512,256]{2,0,1:T(2,128)} %copy.122), calls=%async_computation.6 | async-start | bytes 2097152 | tf_op jit(solution)/shard_map/all_to_all | solution.py:79
  457.3 33.6 %all-to-all-start.7 = ((f32[2,512,256]{2,0,1:T(2,128)}), f32[2,512,256]{2,0,1:T(2,128)S(1)}, u32[]{:S(2)}, u32[]{:S(2)}) async-start(f32[2,512,256]{2,0,1:T(2,128)} %copy.125), calls=%async_computation.7 | async-start | bytes 2097152 | tf_op jit(solution)/shard_map/all_to_all | solution.py:80
  473.3 2.0 copy-start.5
  490.9 19.3 %all-to-all-start.17 = ((f32[32,16,256]{2,1,0:T(8,128)}), f32[32,16,256]{2,1,0:T(8,128)}, u32[]{:S(2)}, u32[]{:S(2)}) async-start(f32[32,16,256]{2,1,0:T(8,128)} %copy.152), calls=%async_computation.17 | async-start | bytes 1048576 | tf_op jit(solution)/shard_map/all_to_all | solution.py:86
  503.8 10.1 %copy-start.4 = (f32[64,16,256]{2,0,1:T(8,128)S(1)}, f32[64,16,256]{2,0,1:T(8,128)}, u32[]{:S(2)}) copy-start(f32[64,16,256]{2,0,1:T(8,128)} %all_to_all.231) | copy-start | bytes 3145732
  510.2 15.3 %all-to-all-start.8 = ((f32[32,16,256]{2,1,0:T(8,128)}), f32[32,16,256]{2,1,0:T(8,128)S(1)}, u32[]{:S(2)}, u32[]{:S(2)}) async-start(f32[32,16,256]{2,1,0:T(8,128)} %copy.128), calls=%async_computation.8 | async-start | bytes 1048576 | tf_op jit(solution)/shard_map/all_to_all | solution.py:86
  525.4 15.3 %all-to-all-start.14 = ((f32[32,16,256]{2,1,0:T(8,128)}), f32[32,16,256]{2,1,0:T(8,128)S(1)}, u32[]{:S(2)}, u32[]{:S(2)}) async-start(f32[32,16,256]{2,1,0:T(8,128)} %copy.145), calls=%async_computation.14 | async-start | bytes 1048576 | tf_op jit(solution)/shard_map/all_to_all | solution.py:86
  529.1 56.2 %all-reduce.2.cloned.1.call-start = ((), (), s32[]{:S(2)}) async-start(), calls=%async_computation.18 | async-start | bytes 1048576 | tf_op jit(solution)/shard_map/psum | solution.py:115
  529.9 10.8 %copy-start.14 = (bf16[1,512,256]{2,1,0:T(8,128)(2,1)S(1)}, bf16[1,512,256]{2,1,0:T(8,128)(2,1)}, u32[]{:S(2)}) copy-start(bf16[1,512,256]{2,1,0:T(8,128)(2,1)} %param.7) | copy-start | bytes 786436
  529.9 10.8 %copy-start.15 = (bf16[1,512,256]{2,1,0:T(8,128)(2,1)S(1)}, bf16[1,512,256]{2,1,0:T(8,128)(2,1)}, u32[]{:S(2)}) copy-start(bf16[1,512,256]{2,1,0:T(8,128)(2,1)} %param.6) | copy-start | bytes 786436
Sparse Core Ops, SparseCore 0:
  532.6 52.6 all-reduce.1
where the time goes:
time: 606 us; the launch traced here: 594 us
  waiting for transfers between devices  231 us (38%)
  matrix products  194 us (32%)
  starting transfers between devices  89 us (15%)
  local copies, waits for them, and re-layouts  61.1 us (10%)
  between operations  14.9 us (2%)
    all_to_all x3, waiting for transfers between devices, inverse_signal(): lax.all_to_all(turned_real, 'seq', split_axis=1, concat_axis=0, tiled=True)  46 us
    psum x1, waiting for transfers between devices, shards(): filter_grad = lax.psum(filter_part, 'dp')  43.8 us
    all_to_all x3, waiting for transfers between devices, forward_spectrum(): lax.all_to_all(imag_b, 'seq', split_axis=0, concat_axis=1, tiled=True)  30.6 us
    all_to_all x3, waiting for transfers between devices, forward_spectrum(): lax.all_to_all(real_b, 'seq', split_axis=0, concat_axis=1, tiled=True)  30.4 us
    all_to_all x3, waiting for transfers between devices, inverse_signal(): lax.all_to_all(turned_imag, 'seq', split_axis=1, concat_axis=0, tiled=True)  30.3 us
    all_to_all x3, waiting for transfers between devices, forward_spectrum(): lax.all_to_all(signal, 'seq', split_axis=0, concat_axis=0, tiled=True)  24.5 us
    all_to_all x3, waiting for transfers between devices, inverse_signal(): lax.all_to_all(values, 'seq', split_axis=0, concat_axis=1, tiled=True)  24.4 us
    dot_general x3, matrix products, forward_spectrum(): jnp.einsum('kj,ajc->akc', fine_sin, real_b, precision=highest_mode)  24.1 us
  transfers between devices with their start and end apart: 19, of which 16 were waited for; matrix products, arithmetic and copies ran while one was open for 21% of the time, Pallas kernels for 0%

commit v1 on v0

v1 whole, which is shorter than its diff:
```python
import functools
import math

import jax
import jax.numpy as jnp
import ml_dtypes
import numpy as np
from jax import lax
from jax.experimental import pallas as pl
from jax.experimental.pallas import tpu as pltpu
from jax.sharding import PartitionSpec as P

MESH = pl.DeviceIdType.MESH
SEQ = 32
DP = 4
LANES = 128
ROWS = 1024
POINTS = 16384
BF = jnp.bfloat16
F32 = jnp.float32


def halves(table):
    table = np.asarray(table, np.float32)
    high = table.astype(ml_dtypes.bfloat16)
    low = (table - high.astype(np.float32)).astype(ml_dtypes.bfloat16)
    return high, low


def make_tables():
    idx = np.arange(LANES, dtype=np.float64)
    turn = 2.0 * math.pi * np.outer(idx + 0.25, idx) / LANES
    first = np.concatenate([np.cos(turn), -np.sin(turn)], axis=0)
    twist = 2.0 * math.pi * np.outer(idx + 0.25, idx) / POINTS
    plain = 2.0 * math.pi * np.outer(idx, idx) / LANES
    cos, sin = np.cos(plain), np.sin(plain)
    second = np.block([[cos, -sin], [sin, cos]])
    back = np.block([[cos, sin], [-sin, cos]])
    last = np.concatenate([np.cos(turn).T, -np.sin(turn).T], axis=1) / POINTS
    first_h, first_l = halves(first)
    first_cat = np.concatenate([first_h, first_h], axis=1)
    second_h, second_l = halves(second)
    back_h, back_l = halves(back)
    last_h, last_l = halves(last)
    return (
        first_cat,
        first_l,
        second_h,
        second_l,
        back_h,
        back_l,
        last_h,
        last_l,
        np.cos(twist).astype(np.float32),
        (-np.sin(twist)).astype(np.float32),
    )


def split(x):
    high = x.astype(BF)
    return high, (x - high.astype(F32)).astype(BF)


def dot(a, b):
    return jnp.dot(a, b, preferred_element_type=F32)


def kernel(
    query, key_in, value, grad, taps,
    first_cat, first_l, second_h, second_l, back_h, back_l, last_h, last_l, turn_re, turn_im,
    out_query, out_key, out_value, out_filter,
    s_gate, s_dgate, s_taps, s_corr, s_conv, s_adj,
    r_gate, r_dgate, r_taps, r_corr, r_conv, r_adj,
    f_gate, f_dgate, f_taps,
    z_part, z_sum, z_full,
    send_sem, recv_sem, z_send, z_recv,
):
    dp = lax.axis_index("dp")
    me = lax.axis_index("seq")
    tp = lax.axis_index("tp")
    chip, core = me // 2, lax.rem(me, 2)
    x_at, y_at = chip // 4, lax.rem(chip, 4)

    def partner(step):
        dc = lax.rem(step, 2)
        dy = lax.rem(step // 2, 4)
        dx = step // 8
        return (lax.rem(x_at + dx, 4) * 4 + lax.rem(y_at + dy, 4)) * 2 + lax.rem(core + dc, 2)

    barrier = pltpu.get_barrier_semaphore()

    @pl.loop(1, SEQ)
    def _(step):
        pl.semaphore_signal(barrier, inc=1, device_id=(dp, partner(step), tp), device_id_type=MESH)

    for step in range(1, DP):
        pl.semaphore_signal(
            barrier, inc=1, device_id=(lax.rem(dp + step, DP), me, tp), device_id_type=MESH
        )

    def pack(out, block):
        for a in range(4):
            for h in range(2):
                tile = block(pl.ds(LANES * a, LANES), pl.ds(LANES * h, LANES)).T
                for d in range(16):
                    out[pl.ds((16 * h + d) * 32 + 8 * a, 8), :] = tile[8 * d : 8 * d + 8, :]

    def unpack(ref, a, h):
        return jnp.concatenate(
            [ref[pl.ds((16 * h + d) * 32 + 8 * a, 8), :] for d in range(16)], axis=0
        ).T

    def exchange(index, src, dst):
        @pl.loop(1, SEQ)
        def _(step):
            to = partner(step)
            pltpu.make_async_remote_copy(
                src_ref=src.at[pl.ds(pl.multiple_of(to * 32, 32), 32)],
                dst_ref=dst.at[pl.ds(pl.multiple_of(me * 32, 32), 32)],
                send_sem=send_sem.at[index],
                recv_sem=recv_sem.at[index],
                device_id=(dp, to, tp),
                device_id_type=MESH,
            ).start()

        mine = pl.ds(pl.multiple_of(me * 32, 32), 32)
        pltpu.make_async_copy(src.at[mine], dst.at[mine], recv_sem.at[index]).start()

    def arrived(index, dst):
        pltpu.make_async_copy(dst, dst, recv_sem.at[index]).wait()

    def sent(index, src):
        part = src.at[pl.ds(0, ROWS - 32)]
        pltpu.make_async_copy(part, part, send_sem.at[index]).wait()

    def forward(src, spec):
        @pl.loop(0, 4)
        def _(pair):
            y = jnp.concatenate(
                [src[pl.ds(2 * pair + j, LANES, stride=8), :] for j in range(2)], axis=1
            )
            yh, yl = split(y)
            a = dot(first_cat[...], jnp.concatenate([yh, yl], axis=0)) + dot(first_l[...], yh)
            rows = []
            for j in range(2):
                re, im = a[:LANES, LANES * j : LANES * (j + 1)], a[LANES:, LANES * j : LANES * (j + 1)]
                wr, wi = turn_re[...], turn_im[...]
                rows.append(jnp.concatenate([re * wr - im * wi, re * wi + im * wr], axis=1))
            ph, pw = split(jnp.concatenate(rows, axis=0))
            spec[pl.ds(pl.multiple_of(pair * 256, 256), 256), :] = (
                dot(ph, second_h[...]) + dot(pw, second_h[...]) + dot(ph, second_l[...])
            )

    def inverse(left, right, conj, dst):
        @pl.loop(0, 4)
        def _(pair):
            at = pl.ds(pl.multiple_of(pair * 256, 256), 256)
            lr, li = left[at, :LANES], left[at, LANES:]
            rr, ri = right[at, :LANES], right[at, LANES:]
            if conj:
                prod = [lr * rr + li * ri, lr * ri - li * rr]
            else:
                prod = [lr * rr - li * ri, lr * ri + li * rr]
            ph, pw = split(jnp.concatenate(prod, axis=1))
            b = dot(ph, back_h[...]) + dot(pw, back_h[...]) + dot(ph, back_l[...])
            cols = []
            for j in range(2):
                re, im = b[LANES * j : LANES * (j + 1), :LANES], b[LANES * j : LANES * (j + 1), LANES:]
                wr, wi = turn_re[...], turn_im[...]
                cols.append(jnp.concatenate([re * wr + im * wi, im * wr - re * wi], axis=0))
            zh, zl = split(jnp.concatenate(cols, axis=1))
            y = dot(last_h[...], zh) + dot(last_h[...], zl) + dot(last_l[...], zh)
            for j in range(2):
                dst[pl.ds(2 * pair + j, LANES, stride=8), :] = y[:, LANES * j : LANES * (j + 1)]

    pack(s_gate, lambda p, c: key_in[0, p, c].astype(F32) * value[0, p, c].astype(F32))
    pl.semaphore_wait(barrier, SEQ + DP - 2)
    exchange(0, s_gate, r_gate)
    pack(s_dgate, lambda p, c: grad[0, p, c].astype(F32) * query[0, p, c].astype(F32))
    exchange(1, s_dgate, r_dgate)
    pack(s_taps, lambda p, c: taps[p, c])
    exchange(2, s_taps, r_taps)

    arrived(0, r_gate)
    forward(r_gate, f_gate)
    arrived(1, r_dgate)
    forward(r_dgate, f_dgate)
    inverse(f_gate, f_dgate, True, s_corr)
    exchange(3, s_corr, r_corr)
    arrived(2, r_taps)
    forward(r_taps, f_taps)
    inverse(f_taps, f_gate, False, s_conv)
    exchange(4, s_conv, r_conv)
    inverse(f_taps, f_dgate, True, s_adj)
    exchange(5, s_adj, r_adj)

    arrived(3, r_corr)
    for step in range(1, DP):
        to = lax.rem(dp + step, DP)
        pltpu.make_async_remote_copy(
            src_ref=r_corr.at[pl.ds(pl.multiple_of(to * 256, 256), 256)],
            dst_ref=z_part.at[step - 1],
            send_sem=z_send.at[0],
            recv_sem=z_recv.at[0],
            device_id=(to, me, tp),
            device_id_type=MESH,
        ).start()
    pltpu.make_async_copy(z_part, z_part, z_recv.at[0]).wait()
    own = pl.ds(pl.multiple_of(dp * 256, 256), 256)
    z_sum[...] = (r_corr[own, :] + z_part[0] + z_part[1] + z_part[2]) * (
        1.0 / math.sqrt(DP * POINTS)
    )
    for step in range(1, DP):
        pltpu.make_async_remote_copy(
            src_ref=z_sum,
            dst_ref=z_full.at[own],
            send_sem=z_send.at[1],
            recv_sem=z_recv.at[1],
            device_id=(lax.rem(dp + step, DP), me, tp),
            device_id_type=MESH,
        ).start()
    pltpu.make_async_copy(z_sum, z_full.at[own], z_recv.at[1]).start()

    arrived(4, r_conv)
    for a in range(4):
        for h in range(2):
            p, c = pl.ds(LANES * a, LANES), pl.ds(LANES * h, LANES)
            out_query[0, p, c] = (grad[0, p, c].astype(F32) * unpack(r_conv, a, h)).astype(BF)
    arrived(5, r_adj)
    for a in range(4):
        for h in range(2):
            p, c = pl.ds(LANES * a, LANES), pl.ds(LANES * h, LANES)
            adjoint = unpack(r_adj, a, h)
            out_key[0, p, c] = (adjoint * value[0, p, c].astype(F32)).astype(BF)
            out_value[0, p, c] = (adjoint * key_in[0, p, c].astype(F32)).astype(BF)
    pltpu.make_async_copy(z_full, z_full, z_recv.at[1]).wait()
    for a in range(4):
        for h in range(2):
            out_filter[pl.ds(LANES * a, LANES), pl.ds(LANES * h, LANES)] = unpack(z_full, a, h)

    for index, src in enumerate((s_gate, s_dgate, s_taps, s_corr, s_conv, s_adj)):
        sent(index, src)
    for index in range(2):
        pltpu.make_async_copy(z_part, z_part, z_send.at[index]).wait()


def shards(query, key_in, value, grad_out, filter_taps):
    vmem = pl.BlockSpec(memory_space=pltpu.VMEM)
    tables = tuple(jnp.asarray(t) for t in make_tables())
    block = pltpu.VMEM((ROWS, LANES), F32)
    return pl.pallas_call(
        kernel,
        out_shape=(
            jax.ShapeDtypeStruct(query.shape, BF),
            jax.ShapeDtypeStruct(query.shape, BF),
            jax.ShapeDtypeStruct(query.shape, BF),
            jax.ShapeDtypeStruct(filter_taps.shape, F32),
        ),
        in_specs=[vmem] * (5 + len(tables)),
        out_specs=(vmem,) * 4,
        scratch_shapes=[block] * 12
        + [pltpu.VMEM((ROWS, 2 * LANES), F32)] * 3
        + [
            pltpu.VMEM((DP - 1, ROWS // DP, LANES), F32),
            pltpu.VMEM((ROWS // DP, LANES), F32),
            block,
            pltpu.SemaphoreType.DMA((6,)),
            pltpu.SemaphoreType.DMA((6,)),
            pltpu.SemaphoreType.DMA((2,)),
            pltpu.SemaphoreType.DMA((2,)),
        ],
        compiler_params=pltpu.CompilerParams(
            collective_id=0, has_side_effects=True, vmem_limit_bytes=48 * 1024 * 1024
        ),
    )(query, key_in, value, grad_out, filter_taps, *tables)


def solution(mesh):
    wide = P("dp", "seq", "tp")
    narrow = P("seq", "tp")
    return jax.shard_map(
        shards,
        mesh=mesh,
        in_specs=(wide, wide, wide, wide, narrow),
        out_specs=(wide, wide, wide, narrow),
        check_vma=False,
    )
```

time: 606 us -> 78.5 us (0.13)
  the two profiles are of different devices: /device:TPU:1 before, /device:TPU:224 now
where the time goes in v1:
time: 78.5 us; the launch traced here: 78 us
  Pallas kernels  60.8 us (77%)
  local copies, waits for them, and re-layouts  16.4 us (21%)
    pallas_call x1, Pallas kernels, shards(): pl.pallas_call(kernel, out_shape=(jax.ShapeDtypeStruct(query.shape, BF),...  60.8 us
    unnamed x34, local copies, waits for them, and re-layouts  16.4 us

profile of v1, /device:TPU:224, one launch (start us, length us, event | category | flops | bytes accessed | tf_op | source)
XLA Modules:
  0.0 78.0 jit_solution(14096757843380151697)
XLA Ops:
  0.6 0.0 copy-start
  0.6 1.0 %copy-done = f32[512,256]{1,0:T(8,128)S(1)} copy-done((f32[512,256]{1,0:T(8,128)S(1)}, f32[512,256]{1,0:T(8,128)}, u32[]{:S(2)}) %copy-start) | copy-done | bytes 524312
  1.7 0.0 copy-start.1
  1.7 0.9 %copy-done.1 = bf16[1,512,256]{2,1,0:T(8,128)(2,1)S(1)} copy-done((bf16[1,512,256]{2,1,0:T(8,128)(2,1)S(1)}, bf16[1,512,256]{2,1,0:T(8,128)(2,1)}, u32[]{:S(2)}) %copy-start.1) | copy-done | bytes 262168
  2.6 0.0 copy-start.2
  2.6 0.9 %copy-done.2 = bf16[1,512,256]{2,1,0:T(8,128)(2,1)S(1)} copy-done((bf16[1,512,256]{2,1,0:T(8,128)(2,1)S(1)}, bf16[1,512,256]{2,1,0:T(8,128)(2,1)}, u32[]{:S(2)}) %copy-start.2) | copy-done | bytes 262168
  3.6 0.0 copy-start.3
  3.6 0.9 %copy-done.3 = bf16[1,512,256]{2,1,0:T(8,128)(2,1)S(1)} copy-done((bf16[1,512,256]{2,1,0:T(8,128)(2,1)S(1)}, bf16[1,512,256]{2,1,0:T(8,128)(2,1)}, u32[]{:S(2)}) %copy-start.3) | copy-done | bytes 262168
  4.5 0.0 copy-start.4
  4.5 0.9 %copy-done.4 = bf16[1,512,256]{2,1,0:T(8,128)(2,1)S(1)} copy-done((bf16[1,512,256]{2,1,0:T(8,128)(2,1)S(1)}, bf16[1,512,256]{2,1,0:T(8,128)(2,1)}, u32[]{:S(2)}) %copy-start.4) | copy-done | bytes 262168
  5.5 0.0 copy-start.5
  5.5 0.9 %copy-done.5 = bf16[256,256]{1,0:T(8,128)(2,1)S(1)} copy-done((bf16[256,256]{1,0:T(8,128)(2,1)S(1)}, bf16[256,256]{1,0:T(8,128)(2,1)}, u32[]{:S(2)}) %copy-start.5) | copy-done | bytes 131096
  6.4 0.0 copy-start.6
  6.4 0.9 %copy-done.6 = bf16[256,256]{1,0:T(8,128)(2,1)S(1)} copy-done((bf16[256,256]{1,0:T(8,128)(2,1)S(1)}, bf16[256,256]{1,0:T(8,128)(2,1)}, u32[]{:S(2)}) %copy-start.6) | copy-done | bytes 131096
  7.3 0.0 copy-start.7
  7.3 0.9 %copy-done.7 = bf16[256,256]{1,0:T(8,128)(2,1)S(1)} copy-done((bf16[256,256]{1,0:T(8,128)(2,1)S(1)}, bf16[256,256]{1,0:T(8,128)(2,1)}, u32[]{:S(2)}) %copy-start.7) | copy-done | bytes 131096
  8.2 0.0 copy-start.8
  8.2 0.9 %copy-done.8 = bf16[256,256]{1,0:T(8,128)(2,1)S(1)} copy-done((bf16[256,256]{1,0:T(8,128)(2,1)S(1)}, bf16[256,256]{1,0:T(8,128)(2,1)}, u32[]{:S(2)}) %copy-start.8) | copy-done | bytes 131096
  9.1 0.0 copy-start.9
  9.1 0.9 %copy-done.9 = bf16[256,256]{1,0:T(8,128)(2,1)S(1)} copy-done((bf16[256,256]{1,0:T(8,128)(2,1)S(1)}, bf16[256,256]{1,0:T(8,128)(2,1)}, u32[]{:S(2)}) %copy-start.9) | copy-done | bytes 131096
  10.0 0.0 copy-start.10
  10.0 0.8 %copy-done.10 = f32[128,128]{1,0:T(8,128)S(1)} copy-done((f32[128,128]{1,0:T(8,128)S(1)}, f32[128,128]{1,0:T(8,128)}, u32[]{:S(2)}) %copy-start.10) | copy-done | bytes 65560
  10.8 0.0 copy-start.11
  10.8 0.8 %copy-done.11 = f32[128,128]{1,0:T(8,128)S(1)} copy-done((f32[128,128]{1,0:T(8,128)S(1)}, f32[128,128]{1,0:T(8,128)}, u32[]{:S(2)}) %copy-start.11) | copy-done | bytes 65560
  11.7 0.0 copy-start.12
  11.7 0.8 %copy-done.12 = bf16[128,256]{1,0:T(8,128)(2,1)S(1)} copy-done((bf16[128,256]{1,0:T(8,128)(2,1)S(1)}, bf16[128,256]{1,0:T(8,128)(2,1)}, u32[]{:S(2)}) %copy-start.12) | copy-done | bytes 65560
  12.5 0.0 copy-start.13
  12.5 0.8 %copy-done.13 = bf16[128,256]{1,0:T(8,128)(2,1)S(1)} copy-done((bf16[128,256]{1,0:T(8,128)(2,1)S(1)}, bf16[128,256]{1,0:T(8,128)(2,1)}, u32[]{:S(2)}) %copy-start.13) | copy-done | bytes 65560
  13.4 0.0 copy-start.14
  13.4 0.8 %copy-done.14 = bf16[256,128]{1,0:T(8,128)(2,1)S(1)} copy-done((bf16[256,128]{1,0:T(8,128)(2,1)S(1)}, bf16[256,128]{1,0:T(8,128)(2,1)}, u32[]{:S(2)}) %copy-start.14) | copy-done | bytes 65560
  14.2 60.8 %shard_map.174 = (bf16[1,512,256]{2,1,0:T(8,128)(2,1)S(1)}, bf16[1,512,256]{2,1,0:T(8,128)(2,1)S(1)}, bf16[1,512,256]{2,1,0:T(8,128)(2,1)S(1)}, f32[512,256]{1,0:T(8,128)S(1)}) custom-call(bf16[1,512,256]{2,1,0:T(8,128)(2,1)S(1)} %copy-done.1, bf16[1,512,256]{2,1,0:T(8,128)(2,1)S(1)} %copy-done.2, bf16[1,512,256]{2,1,0:T(8,128)(2,1)S(1)} %copy-done.3, ...), custom_call_target="tpu_custom_call" | custom-call | tf_op jit(solution)/shard_map/pallas_call | solution.py:251
  75.0 0.7 copy.23
  75.8 0.7 copy.24
  76.5 0.7 copy.25
  77.2 0.8 %copy.26 = f32[512,256]{1,0:T(8,128)} copy(f32[512,256]{1,0:T(8,128)S(1)} %get-tuple-element.11) | data formatting | bytes 1048576
Async XLA Ops:
  0.6 1.0 %copy-start = (f32[512,256]{1,0:T(8,128)S(1)}, f32[512,256]{1,0:T(8,128)}, u32[]{:S(2)}) copy-start(f32[512,256]{1,0:T(8,128)} %taps.1) | copy-start | bytes 1572868
  1.7 0.9 %copy-start.1 = (bf16[1,512,256]{2,1,0:T(8,128)(2,1)S(1)}, bf16[1,512,256]{2,1,0:T(8,128)(2,1)}, u32[]{:S(2)}) copy-start(bf16[1,512,256]{2,1,0:T(8,128)(2,1)} %query.1) | copy-start | bytes 786436
  2.6 0.9 %copy-start.2 = (bf16[1,512,256]{2,1,0:T(8,128)(2,1)S(1)}, bf16[1,512,256]{2,1,0:T(8,128)(2,1)}, u32[]{:S(2)}) copy-start(bf16[1,512,256]{2,1,0:T(8,128)(2,1)} %key_in.1) | copy-start | bytes 786436
  3.6 0.9 %copy-start.3 = (bf16[1,512,256]{2,1,0:T(8,128)(2,1)S(1)}, bf16[1,512,256]{2,1,0:T(8,128)(2,1)}, u32[]{:S(2)}) copy-start(bf16[1,512,256]{2,1,0:T(8,128)(2,1)} %value.1) | copy-start | bytes 786436
  4.5 0.9 %copy-start.4 = (bf16[1,512,256]{2,1,0:T(8,128)(2,1)S(1)}, bf16[1,512,256]{2,1,0:T(8,128)(2,1)}, u32[]{:S(2)}) copy-start(bf16[1,512,256]{2,1,0:T(8,128)(2,1)} %grad.1) | copy-start | bytes 786436
  5.5 0.9 %copy-start.5 = (bf16[256,256]{1,0:T(8,128)(2,1)S(1)}, bf16[256,256]{1,0:T(8,128)(2,1)}, u32[]{:S(2)}) copy-start(bf16[256,256]{1,0:T(8,128)(2,1)} %constant.25.clone.back_l) | copy-start | bytes 393220
  6.4 0.9 %copy-start.6 = (bf16[256,256]{1,0:T(8,128)(2,1)S(1)}, bf16[256,256]{1,0:T(8,128)(2,1)}, u32[]{:S(2)}) copy-start(bf16[256,256]{1,0:T(8,128)(2,1)} %constant.24.clone.back_h) | copy-start | bytes 393220
  7.3 0.9 %copy-start.7 = (bf16[256,256]{1,0:T(8,128)(2,1)S(1)}, bf16[256,256]{1,0:T(8,128)(2,1)}, u32[]{:S(2)}) copy-start(bf16[256,256]{1,0:T(8,128)(2,1)} %constant.23.clone.second_l) | copy-start | bytes 393220
  8.2 0.9 %copy-start.8 = (bf16[256,256]{1,0:T(8,128)(2,1)S(1)}, bf16[256,256]{1,0:T(8,128)(2,1)}, u32[]{:S(2)}) copy-start(bf16[256,256]{1,0:T(8,128)(2,1)} %constant.22.clone.second_h) | copy-start | bytes 393220
  9.1 0.9 %copy-start.9 = (bf16[256,256]{1,0:T(8,128)(2,1)S(1)}, bf16[256,256]{1,0:T(8,128)(2,1)}, u32[]{:S(2)}) copy-start(bf16[256,256]{1,0:T(8,128)(2,1)} %constant.20.clone.first_cat) | copy-start | bytes 393220
  10.0 0.8 %copy-start.10 = (f32[128,128]{1,0:T(8,128)S(1)}, f32[128,128]{1,0:T(8,128)}, u32[]{:S(2)}) copy-start(f32[128,128]{1,0:T(8,128)} %constant.29.clone.turn_im) | copy-start | bytes 196612
  10.8 0.8 %copy-start.11 = (f32[128,128]{1,0:T(8,128)S(1)}, f32[128,128]{1,0:T(8,128)}, u32[]{:S(2)}) copy-start(f32[128,128]{1,0:T(8,128)} %constant.28.clone.turn_re) | copy-start | bytes 196612
  11.7 0.8 %copy-start.12 = (bf16[128,256]{1,0:T(8,128)(2,1)S(1)}, bf16[128,256]{1,0:T(8,128)(2,1)}, u32[]{:S(2)}) copy-start(bf16[128,256]{1,0:T(8,128)(2,1)} %constant.27.clone.last_l) | copy-start | bytes 196612
  12.5 0.8 %copy-start.13 = (bf16[128,256]{1,0:T(8,128)(2,1)S(1)}, bf16[128,256]{1,0:T(8,128)(2,1)}, u32[]{:S(2)}) copy-start(bf16[128,256]{1,0:T(8,128)(2,1)} %constant.26.clone.last_h) | copy-start | bytes 196612
  13.4 0.8 %copy-start.14 = (bf16[256,128]{1,0:T(8,128)(2,1)S(1)}, bf16[256,128]{1,0:T(8,128)(2,1)}, u32[]{:S(2)}) copy-start(bf16[256,128]{1,0:T(8,128)(2,1)} %constant.21.clone.first_l) | copy-start | bytes 196612

commit v2 on v1

v2 whole, which is shorter than its diff:
```python
import functools
import math

import jax
import jax.numpy as jnp
import ml_dtypes
import numpy as np
from jax import lax
from jax.experimental import pallas as pl
from jax.experimental.pallas import tpu as pltpu
from jax.sharding import PartitionSpec as P

MESH = pl.DeviceIdType.MESH
SEQ = 32
DP = 4
LANES = 128
ROWS = 1024
POINTS = 16384
BF = jnp.bfloat16
F32 = jnp.float32


def halves(table):
    table = np.asarray(table, np.float32)
    high = table.astype(ml_dtypes.bfloat16)
    low = (table - high.astype(np.float32)).astype(ml_dtypes.bfloat16)
    return high, low


def make_tables():
    idx = np.arange(LANES, dtype=np.float64)
    turn = 2.0 * math.pi * np.outer(idx + 0.25, idx) / LANES
    first = np.concatenate([np.cos(turn), -np.sin(turn)], axis=0)
    twist = 2.0 * math.pi * np.outer(idx + 0.25, idx) / POINTS
    plain = 2.0 * math.pi * np.outer(idx, idx) / LANES
    cos, sin = np.cos(plain), np.sin(plain)
    second = np.block([[cos, -sin], [sin, cos]])
    back = np.block([[cos, sin], [-sin, cos]])
    last = np.concatenate([np.cos(turn).T, -np.sin(turn).T], axis=1) / POINTS
    first_h, first_l = halves(first)
    mats = [
        np.concatenate([first_h, first_h], axis=1),
        np.concatenate([first_l, np.zeros_like(first_l)], axis=1),
        *halves(second),
        *halves(back),
        *halves(last),
    ]
    turns = [np.cos(twist), -np.sin(twist)]
    return np.concatenate(mats, axis=0), np.concatenate(turns, axis=0).astype(np.float32)


def split(x):
    high = x.astype(BF)
    return high, (x - high.astype(F32)).astype(BF)


def dot(a, b):
    return jnp.dot(a, b, preferred_element_type=F32)


def kernel(
    query_in, key_hbm, value_in, grad_in, taps_in, mats_in, turns_in,
    out_query, out_key, out_value, out_filter,
    query, key_in, value, grad, taps, mats, turns,
    o_query, o_key, o_value, o_filter,
    t_gd, t_taps, t_corr, t_ret, t_filt,
    s_gd, r_gd, s_taps, r_taps, s_ret, r_ret,
    f_gd, f_taps, c_part, z_part, z_sum, z_all,
    x_send, x_recv, m_send, m_recv, rs_send, rs_recv, ag_send, ag_recv,
    pair_send, pair_recv, load_sem, store_sem,
):
    dp = lax.axis_index("dp")
    me = lax.axis_index("seq")
    tp = lax.axis_index("tp")
    chip, core = me // 2, lax.rem(me, 2)
    x_at, y_at = chip // 4, lax.rem(chip, 4)
    odd = lax.rem(dp, 2)
    mate = dp + 1 - 2 * odd

    loads = [
        pltpu.make_async_copy(src, dst, load_sem.at[i])
        for i, (src, dst) in enumerate(
            (
                (key_hbm, key_in),
                (value_in, value),
                (grad_in, grad),
                (query_in, query),
                (taps_in, taps),
                (mats_in, mats),
                (turns_in, turns),
            )
        )
    ]
    for load in loads:
        load.start()
    first_cat = mats.at[pl.ds(0, 256)]
    first_l = mats.at[pl.ds(256, 256), pl.ds(0, LANES)]
    second_h, second_l, back_h, back_l = (mats.at[pl.ds(512 + 256 * i, 256)] for i in range(4))
    last_h, last_l = (mats.at[pl.ds(1536 + LANES * i, LANES)] for i in range(2))
    turn_re, turn_im = (turns.at[pl.ds(LANES * i, LANES)] for i in range(2))

    def partner(step):
        dc = lax.rem(step, 2)
        dy = lax.rem(step // 2, 4)
        dx = step // 8
        return (lax.rem(x_at + dx, 4) * 4 + lax.rem(y_at + dy, 4)) * 2 + lax.rem(core + dc, 2)

    barrier = pltpu.get_barrier_semaphore()

    @pl.loop(1, SEQ)
    def _(step):
        pl.semaphore_signal(barrier, inc=1, device_id=(dp, partner(step), tp), device_id_type=MESH)

    for step in range(1, DP):
        pl.semaphore_signal(
            barrier, inc=1, device_id=(lax.rem(dp + step, DP), me, tp), device_id_type=MESH
        )


    def exchange(index, src, dst, base):
        mine = pl.ds(pl.multiple_of(base + me * 16, 16), 16)

        @pl.loop(1, SEQ)
        def _(step):
            to = partner(step)
            pltpu.make_async_remote_copy(
                src_ref=src.at[pl.ds(pl.multiple_of(base + to * 16, 16), 16)],
                dst_ref=dst.at[mine],
                send_sem=x_send.at[index],
                recv_sem=x_recv.at[index],
                device_id=(dp, to, tp),
                device_id_type=MESH,
            ).start()

        pltpu.make_async_copy(src.at[mine], dst.at[mine], x_recv.at[index]).start()

    def arrived(index, dst, base):
        part = dst.at[pl.ds(pl.multiple_of(base, 512), 512)]
        pltpu.make_async_copy(part, part, x_recv.at[index]).wait()


    def transpose_gd(h):
        c = pl.ds(LANES * h, LANES)
        for sig, (left, right) in enumerate(((key_in, value), (grad, query))):
            for a in range(4):
                p = pl.ds(LANES * a, LANES)
                at = ((h * 2 + sig) * 4 + a) * LANES
                t_gd[pl.ds(at, LANES), :] = (left[0, p, c].astype(F32) * right[0, p, c].astype(F32)).T

    def pack_gd(p):
        for sig in range(2):
            for a in range(4):
                at = (((p // 2) * 2 + sig) * 4 + a) * LANES + 64 * (p % 2)
                for c in range(2):
                    s_gd[pl.ds(p * 512 + a * 4 + sig * 2 + c, 32, stride=16), :] = t_gd[
                        pl.ds(at + c, 32, stride=2), :
                    ]

    def pack_taps():
        for h in range(2):
            for a in range(4):
                at = (h * 4 + a) * LANES
                t_taps[pl.ds(at, LANES), :] = taps[pl.ds(LANES * a, LANES), pl.ds(LANES * h, LANES)].T
        for h in range(2):
            for a in range(4):
                at = (h * 4 + a) * LANES
                for c in range(2):
                    s_taps[pl.ds(a * 4 + h * 2 + c, 32, stride=16), :] = t_taps[
                        pl.ds(at + 64 * odd + c, 32, stride=2), :
                    ]


    def forward(src, base):
        y = jnp.concatenate([src[pl.ds(base + j, LANES, stride=4), :] for j in range(2)], axis=1)
        yh, yl = split(y)
        a = dot(first_cat[...], jnp.concatenate([yh, yl], axis=0)) + dot(first_l[...], yh)
        wr, wi = turn_re[...], turn_im[...]
        rows = []
        for j in range(2):
            re, im = a[:LANES, LANES * j : LANES * (j + 1)], a[LANES:, LANES * j : LANES * (j + 1)]
            rows.append(jnp.concatenate([re * wr - im * wi, re * wi + im * wr], axis=1))
        ph, pw = split(jnp.concatenate(rows, axis=0))
        return dot(ph, second_h[...]) + dot(pw, second_h[...]) + dot(ph, second_l[...])

    def inverse(left, right, conj):
        lr, li, rr, ri = left[:, :LANES], left[:, LANES:], right[:, :LANES], right[:, LANES:]
        if conj:
            prod = [lr * rr + li * ri, lr * ri - li * rr]
        else:
            prod = [lr * rr - li * ri, lr * ri + li * rr]
        ph, pw = split(jnp.concatenate(prod, axis=1))
        b = dot(ph, back_h[...]) + dot(pw, back_h[...]) + dot(ph, back_l[...])
        wr, wi = turn_re[...], turn_im[...]
        cols = []
        for j in range(2):
            re, im = b[LANES * j : LANES * (j + 1), :LANES], b[LANES * j : LANES * (j + 1), LANES:]
            cols.append(jnp.concatenate([re * wr + im * wi, im * wr - re * wi], axis=0))
        zh, zl = split(jnp.concatenate(cols, axis=1))
        return dot(last_h[...], zh) + dot(last_h[...], zl) + dot(last_l[...], zh)

    def spec_at(p, sig):
        return pl.ds(pl.multiple_of((p * 2 + sig) * 256, 256), 256)

    def gate_chunk(p):
        gate = forward(r_gd, p * 512)
        dgate = forward(r_gd, p * 512 + 2)
        f_gd[spec_at(p, 0), :] = gate
        f_gd[spec_at(p, 1), :] = dgate
        y = inverse(gate, dgate, True)
        for c in range(2):
            at = (p * 2 + c) * LANES
            t_corr[pl.ds(at, LANES), :] = y[:, LANES * c : LANES * (c + 1)]
            for a in range(4):
                c_part[pl.ds(p * 256 + a * 64 + c, 32, stride=2), :] = t_corr[
                    pl.ds(at + a, 32, stride=4), :
                ]
        for step in range(1, DP):
            to = lax.rem(dp + step, DP)
            pltpu.make_async_remote_copy(
                src_ref=c_part.at[pl.ds(pl.multiple_of(p * 256 + to * 64, 64), 64)],
                dst_ref=z_part.at[pl.ds((p * 3 + step - 1) * 64, 64)],
                send_sem=rs_send.at[p],
                recv_sem=rs_recv.at[p],
                device_id=(to, me, tp),
                device_id_type=MESH,
            ).start()

    def sum_chunk(p):
        part = z_part.at[pl.ds(p * 192, 192)]
        pltpu.make_async_copy(part, part, rs_recv.at[p]).wait()
        scale = 1.0 / math.sqrt(DP * POINTS)
        for c in range(2):
            total = c_part[pl.ds(p * 256 + dp * 64 + c, 32, stride=2), :]
            for step in range(DP - 1):
                total = total + z_part[pl.ds((p * 3 + step) * 64 + c, 32, stride=2), :]
            z_sum[:, 2 * p + c, :] = total * scale
        two = pl.ds(2 * p, 2)

        @pl.loop(1, SEQ)
        def _(step):
            to = partner(step)
            pltpu.make_async_remote_copy(
                src_ref=z_sum.at[to, two],
                dst_ref=z_all.at[dp, me, two],
                send_sem=m_send.at[p],
                recv_sem=m_recv.at[p],
                device_id=(dp, to, tp),
                device_id_type=MESH,
            ).start()

        pltpu.make_async_copy(z_sum.at[me, two], z_all.at[dp, me, two], m_recv.at[p]).start()

    def spread_chunk(p):
        part = z_all.at[dp, :, pl.ds(2 * p, 2)]
        pltpu.make_async_copy(part, part, m_recv.at[p]).wait()
        for step in range(1, DP):
            pltpu.make_async_remote_copy(
                src_ref=part,
                dst_ref=part,
                send_sem=ag_send.at[p],
                recv_sem=ag_recv.at[p],
                device_id=(lax.rem(dp + step, DP), me, tp),
                device_id_type=MESH,
            ).start()

    def forward_taps(half):
        base = pl.multiple_of(half * 512, 512)
        for h in range(2):
            f_taps[pl.ds(pl.multiple_of((2 * h + half) * 256, 256), 256), :] = forward(
                r_taps, base + 2 * h
            )

    def return_chunk(p):
        filt = f_taps[pl.ds(pl.multiple_of(p * 256, 256), 256), :]
        conv = inverse(filt, f_gd[spec_at(p, 0), :], False)
        adj = inverse(filt, f_gd[spec_at(p, 1), :], True)
        for v in range(4):
            y = (conv, adj)[v // 2]
            s_ret[pl.ds(p * 512 + v, LANES, stride=4), :] = y[:, LANES * (v % 2) : LANES * (v % 2 + 1)]
        exchange(5 + p, s_ret, r_ret, p * 512)

    def unpack_chunk(h, part):
        p = 2 * h + part
        arrived(5 + p, r_ret, p * 512)
        for sig in range(2):
            for a in range(4):
                for c in range(2):
                    t_ret[
                        pl.ds(((h * 2 + sig) * 4 + a) * LANES + 64 * part + c, 32, stride=2), :
                    ] = r_ret[pl.ds(p * 512 + a * 4 + sig * 2 + c, 32, stride=16), :]

    stores = []

    def finish(h):
        c = pl.ds(LANES * h, LANES)
        for a in range(4):
            p = pl.ds(LANES * a, LANES)
            conv = t_ret[pl.ds(((h * 2 + 0) * 4 + a) * LANES, LANES), :].T
            adj = t_ret[pl.ds(((h * 2 + 1) * 4 + a) * LANES, LANES), :].T
            o_query[0, p, c] = (grad[0, p, c].astype(F32) * conv).astype(BF)
            o_key[0, p, c] = (adj * value[0, p, c].astype(F32)).astype(BF)
            o_value[0, p, c] = (adj * key_in[0, p, c].astype(F32)).astype(BF)
        for i, (src, dst) in enumerate(
            ((o_query, out_query), (o_key, out_key), (o_value, out_value))
        ):
            store = pltpu.make_async_copy(src.at[:, :, c], dst.at[:, :, c], store_sem.at[2 * i + h])
            store.start()
            stores.append(store)

    own_taps = r_taps.at[pl.ds(pl.multiple_of(odd * 512, 512), 512)]
    other_taps = r_taps.at[pl.ds(pl.multiple_of((1 - odd) * 512, 512), 512)]
    loads[0].wait()
    loads[1].wait()
    loads[2].wait()
    loads[3].wait()
    transpose_gd(0)
    pack_gd(0)
    pl.semaphore_wait(barrier, SEQ + DP - 2)
    exchange(0, s_gd, r_gd, 0)
    loads[4].wait()
    pack_taps()
    exchange(4, s_taps, own_taps, 0)
    pack_gd(1)
    exchange(1, s_gd, r_gd, 512)
    transpose_gd(1)
    pack_gd(2)
    exchange(2, s_gd, r_gd, 1024)
    pack_gd(3)
    loads[5].wait()
    loads[6].wait()

    arrived(0, r_gd, 0)
    gate_chunk(0)
    exchange(3, s_gd, r_gd, 1536)

    arrived(4, own_taps, 0)
    pair = pltpu.make_async_remote_copy(
        src_ref=own_taps,
        dst_ref=own_taps,
        send_sem=pair_send,
        recv_sem=pair_recv,
        device_id=(mate, me, tp),
        device_id_type=MESH,
    )
    pair.start()
    forward_taps(odd)

    arrived(1, r_gd, 512)
    gate_chunk(1)
    sum_chunk(0)
    return_chunk(odd)

    arrived(2, r_gd, 1024)
    gate_chunk(2)
    sum_chunk(1)
    pltpu.make_async_copy(other_taps, other_taps, pair_recv).wait()
    forward_taps(1 - odd)
    return_chunk(1 - odd)

    arrived(3, r_gd, 1536)
    gate_chunk(3)
    sum_chunk(2)
    spread_chunk(0)
    return_chunk(2 + odd)
    spread_chunk(1)
    return_chunk(3 - odd)
    sum_chunk(3)
    unpack_chunk(0, odd)
    spread_chunk(2)
    unpack_chunk(0, 1 - odd)
    finish(0)
    spread_chunk(3)
    unpack_chunk(1, odd)
    unpack_chunk(1, 1 - odd)
    finish(1)

    for p in range(4):
        part = z_all.at[pl.ds(0, DP - 1), :, pl.ds(2 * p, 2)]
        pltpu.make_async_copy(part, part, ag_recv.at[p]).wait()
        for a in range(4):
            for c in range(2):
                t_filt[
                    pl.ds(((p // 2) * 4 + a) * LANES + 64 * (p % 2) + c, 32, stride=2), :
                ] = z_all[a, :, 2 * p + c, :]
    for h in range(2):
        for a in range(4):
            o_filter[pl.ds(LANES * a, LANES), pl.ds(LANES * h, LANES)] = t_filt[
                pl.ds((h * 4 + a) * LANES, LANES), :
            ].T
    store = pltpu.make_async_copy(o_filter, out_filter, store_sem.at[6])
    store.start()
    stores.append(store)

    pair.wait_send()
    for index in range(9):
        part = s_gd.at[pl.ds(0, 496)]
        pltpu.make_async_copy(part, part, x_send.at[index]).wait()
    for p in range(4):
        part = z_sum.at[pl.ds(0, SEQ - 1), pl.ds(0, 2)]
        pltpu.make_async_copy(part, part, m_send.at[p]).wait()
        part = z_part.at[pl.ds(0, 192)]
        pltpu.make_async_copy(part, part, rs_send.at[p]).wait()
        part = z_all.at[pl.ds(0, DP - 1), :, pl.ds(0, 2)]
        pltpu.make_async_copy(part, part, ag_send.at[p]).wait()
    for store in stores:
        store.wait()


def shards(query, key_in, value, grad_out, filter_taps):
    tables = tuple(jnp.asarray(t) for t in make_tables())
    operands = (query, key_in, value, grad_out, filter_taps, *tables)
    results = (
        jax.ShapeDtypeStruct(query.shape, BF),
        jax.ShapeDtypeStruct(query.shape, BF),
        jax.ShapeDtypeStruct(query.shape, BF),
        jax.ShapeDtypeStruct(filter_taps.shape, F32),
    )

    def block(rows, lanes=LANES):
        return pltpu.VMEM((rows, lanes), F32)

    return pl.pallas_call(
        kernel,
        out_shape=results,
        in_specs=[pl.BlockSpec(memory_space=pl.ANY)] * 7,
        out_specs=(pl.BlockSpec(memory_space=pl.ANY),) * 4,
        scratch_shapes=[pltpu.VMEM(x.shape, x.dtype) for x in operands + results]
        + [block(2048), block(1024), block(1024), block(2048), block(1024)]
        + [block(2048), block(2048), block(512), block(1024), block(2048), block(2048)]
        + [block(2048, 2 * LANES), block(1024, 2 * LANES), block(1024), block(768)]
        + [pltpu.VMEM((SEQ, 8, LANES), F32), pltpu.VMEM((DP, SEQ, 8, LANES), F32)]
        + [pltpu.SemaphoreType.DMA((n,)) for n in (9, 9, 4, 4, 4, 4, 4, 4)]
        + [pltpu.SemaphoreType.DMA] * 2
        + [pltpu.SemaphoreType.DMA((7,)), pltpu.SemaphoreType.DMA((7,))],
        compiler_params=pltpu.CompilerParams(
            collective_id=0, has_side_effects=True, vmem_limit_bytes=60 * 1024 * 1024
        ),
    )(*operands)


def solution(mesh):
    wide = P("dp", "seq", "tp")
    narrow = P("seq", "tp")
    return jax.shard_map(
        shards,
        mesh=mesh,
        in_specs=(wide, wide, wide, wide, narrow),
        out_specs=(wide, wide, wide, narrow),
        check_vma=False,
    )
```

time: 78.5 us -> 56.9 us (0.72)
  the two profiles are of different devices: /device:TPU:224 before, /device:TPU:1 now
where the time goes in v2:
time: 56.9 us; the launch traced here: 56.7 us
  Pallas kernels  52.1 us (92%)
  local copies, waits for them, and re-layouts  3.94 us (7%)
  between operations  0.66 us (1%)
    pallas_call x1, Pallas kernels, shards(): pl.pallas_call(kernel, out_shape=results, in_specs=[pl.BlockSpec(memory_s...  52.1 us
    unnamed x10, local copies, waits for them, and re-layouts  3.94 us

profile of v2, /device:TPU:1, one launch (start us, length us, event | category | flops | bytes accessed | tf_op | source)
XLA Modules:
  0.0 56.7 jit_solution(10020468896724195977)
XLA Ops:
  0.6 52.1 %shard_map.102 = (bf16[1,512,256]{2,1,0:T(8,128)(2,1)}, bf16[1,512,256]{2,1,0:T(8,128)(2,1)}, bf16[1,512,256]{2,1,0:T(8,128)(2,1)}, f32[512,256]{1,0:T(8,128)}) custom-call(bf16[1,512,256]{2,1,0:T(8,128)(2,1)} %query_in.1, bf16[1,512,256]{2,1,0:T(8,128)(2,1)} %key_hbm.1, bf16[1,512,256]{2,1,0:T(8,128)(2,1)} %value_in.1, bf16[1,512,256]{2,1,0:T(8,128)(2,1)} %grad_in.1, ...), custom_call_target="tpu_custom_call" | custom-call | tf_op jit(solution)/shard_map/pallas_call | solution.py:422
  52.8 0.0 copy-start.2
  52.8 0.0 copy-start.1
  52.8 1.7 %copy.15 = bf16[1,512,256]{2,1,0:T(8,128)(2,1)} copy(bf16[1,512,256]{2,1,0:T(8,128)(2,1)} %get-tuple-element.8) | data formatting | bytes 524288
  54.5 0.0 copy-done.2
  54.5 0.0 copy-start
  54.5 0.7 %copy.16 = bf16[1,512,256]{2,1,0:T(8,128)(2,1)} copy(bf16[1,512,256]{2,1,0:T(8,128)(2,1)S(1)} %copy-done.2) | data formatting | bytes 524288
  55.2 0.0 copy-done.1
  55.2 0.7 %copy.17 = bf16[1,512,256]{2,1,0:T(8,128)(2,1)} copy(bf16[1,512,256]{2,1,0:T(8,128)(2,1)S(1)} %copy-done.1) | data formatting | bytes 524288
  55.9 0.0 copy-done
  55.9 0.8 %copy.18 = f32[512,256]{1,0:T(8,128)} copy(f32[512,256]{1,0:T(8,128)S(1)} %copy-done) | data formatting | bytes 1048576
Async XLA Ops:
  52.8 1.7 %copy-start.2 = (bf16[1,512,256]{2,1,0:T(8,128)(2,1)S(1)}, bf16[1,512,256]{2,1,0:T(8,128)(2,1)}, u32[]{:S(2)}) copy-start(bf16[1,512,256]{2,1,0:T(8,128)(2,1)} %get-tuple-element.9) | copy-start | bytes 786436
  52.8 2.4 %copy-start.1 = (bf16[1,512,256]{2,1,0:T(8,128)(2,1)S(1)}, bf16[1,512,256]{2,1,0:T(8,128)(2,1)}, u32[]{:S(2)}) copy-start(bf16[1,512,256]{2,1,0:T(8,128)(2,1)} %get-tuple-element.10) | copy-start | bytes 786436
  54.5 1.4 %copy-start = (f32[512,256]{1,0:T(8,128)S(1)}, f32[512,256]{1,0:T(8,128)}, u32[]{:S(2)}) copy-start(f32[512,256]{1,0:T(8,128)} %get-tuple-element.11) | copy-start | bytes 1572868

commit v3 on v2

--- a/solution.py
+++ b/solution.py
@@ -99,17 +99,15 @@
     last_h, last_l = (mats.at[pl.ds(1536 + LANES * i, LANES)] for i in range(2))
     turn_re, turn_im = (turns.at[pl.ds(LANES * i, LANES)] for i in range(2))
 
-    def partner(step):
-        dc = lax.rem(step, 2)
-        dy = lax.rem(step // 2, 4)
-        dx = step // 8
-        return (lax.rem(x_at + dx, 4) * 4 + lax.rem(y_at + dy, 4)) * 2 + lax.rem(core + dc, 2)
+    at_x = [lax.rem(x_at + d, 4) * 8 for d in (2, 3, 1, 0)]
+    at_y = [lax.rem(y_at + d, 4) * 2 for d in (2, 3, 1, 0)]
+    at_core = [1 - core, core]
+    partners = [x + y + c for c in at_core for x in at_x for y in at_y][:-1]
 
     barrier = pltpu.get_barrier_semaphore()
 
-    @pl.loop(1, SEQ)
-    def _(step):
-        pl.semaphore_signal(barrier, inc=1, device_id=(dp, partner(step), tp), device_id_type=MESH)
+    for to in partners:
+        pl.semaphore_signal(barrier, inc=1, device_id=(dp, to, tp), device_id_type=MESH)
 
     for step in range(1, DP):
         pl.semaphore_signal(
@@ -120,9 +118,7 @@
     def exchange(index, src, dst, base):
         mine = pl.ds(pl.multiple_of(base + me * 16, 16), 16)
 
-        @pl.loop(1, SEQ)
-        def _(step):
-            to = partner(step)
+        for to in partners:
             pltpu.make_async_remote_copy(
                 src_ref=src.at[pl.ds(pl.multiple_of(base + to * 16, 16), 16)],
                 dst_ref=dst.at[mine],
@@ -236,9 +232,7 @@
             z_sum[:, 2 * p + c, :] = total * scale
         two = pl.ds(2 * p, 2)
 
-        @pl.loop(1, SEQ)
-        def _(step):
-            to = partner(step)
+        for to in partners:
             pltpu.make_async_remote_copy(
                 src_ref=z_sum.at[to, two],
                 dst_ref=z_all.at[dp, me, two],
@@ -277,6 +271,8 @@
         for v in range(4):
             y = (conv, adj)[v // 2]
             s_ret[pl.ds(p * 512 + v, LANES, stride=4), :] = y[:, LANES * (v % 2) : LANES * (v % 2 + 1)]
+
+    def send_chunk(p):
         exchange(5 + p, s_ret, r_ret, p * 512)
 
     def unpack_chunk(h, part):
@@ -288,8 +284,6 @@
                     t_ret[
                         pl.ds(((h * 2 + sig) * 4 + a) * LANES + 64 * part + c, 32, stride=2), :
                     ] = r_ret[pl.ds(p * 512 + a * 4 + sig * 2 + c, 32, stride=16), :]
-
-    stores = []
 
     def finish(h):
         c = pl.ds(LANES * h, LANES)
@@ -307,6 +301,7 @@
             store.start()
             stores.append(store)
 
+    stores = []
     own_taps = r_taps.at[pl.ds(pl.multiple_of(odd * 512, 512), 512)]
     other_taps = r_taps.at[pl.ds(pl.multiple_of((1 - odd) * 512, 512), 512)]
     loads[0].wait()
@@ -326,13 +321,11 @@
     pack_gd(2)
     exchange(2, s_gd, r_gd, 1024)
     pack_gd(3)
+    exchange(3, s_gd, r_gd, 1536)
     loads[5].wait()
     loads[6].wait()
-
     arrived(0, r_gd, 0)
     gate_chunk(0)
-    exchange(3, s_gd, r_gd, 1536)
-
     arrived(4, own_taps, 0)
     pair = pltpu.make_async_remote_copy(
         src_ref=own_taps,
@@ -344,29 +337,30 @@
     )
     pair.start()
     forward_taps(odd)
-
     arrived(1, r_gd, 512)
     gate_chunk(1)
+    return_chunk(odd)
+    send_chunk(odd)
     sum_chunk(0)
-    return_chunk(odd)
-
     arrived(2, r_gd, 1024)
     gate_chunk(2)
-    sum_chunk(1)
     pltpu.make_async_copy(other_taps, other_taps, pair_recv).wait()
     forward_taps(1 - odd)
     return_chunk(1 - odd)
-
+    send_chunk(1 - odd)
+    sum_chunk(1)
+    spread_chunk(0)
     arrived(3, r_gd, 1536)
     gate_chunk(3)
+    return_chunk(2 + odd)
+    send_chunk(2 + odd)
     sum_chunk(2)
-    spread_chunk(0)
-    return_chunk(2 + odd)
     spread_chunk(1)
     return_chunk(3 - odd)
     sum_chunk(3)
+    send_chunk(3 - odd)
+    spread_chunk(2)
     unpack_chunk(0, odd)
-    spread_chunk(2)
     unpack_chunk(0, 1 - odd)
     finish(0)
     spread_chunk(3)
@@ -387,6 +381,7 @@
             o_filter[pl.ds(LANES * a, LANES), pl.ds(LANES * h, LANES)] = t_filt[
                 pl.ds((h * 4 + a) * LANES, LANES), :
             ].T
+
     store = pltpu.make_async_copy(o_filter, out_filter, store_sem.at[6])
     store.start()
     stores.append(store)
@@ -406,6 +401,19 @@
         store.wait()
 
 
+def store_kernel(*refs):
+    ins, outs, held = refs[:4], refs[4:8], refs[8:12]
+    loads = [pltpu.make_async_copy(ins[i], held[i], refs[12].at[i]) for i in range(4)]
+    stores = [pltpu.make_async_copy(held[i], outs[i], refs[13].at[i]) for i in range(4)]
+    for load in loads:
+        load.start()
+    for load, store in zip(loads, stores):
+        load.wait()
+        store.start()
+    for store in stores:
+        store.wait()
+
+
 def shards(query, key_in, value, grad_out, filter_taps):
     tables = tuple(jnp.asarray(t) for t in make_tables())
     operands = (query, key_in, value, grad_out, filter_taps, *tables)
@@ -419,7 +427,7 @@
     def block(rows, lanes=LANES):
         return pltpu.VMEM((rows, lanes), F32)
 
-    return pl.pallas_call(
+    outs = pl.pallas_call(
         kernel,
         out_shape=results,
         in_specs=[pl.BlockSpec(memory_space=pl.ANY)] * 7,
@@ -433,9 +441,20 @@
         + [pltpu.SemaphoreType.DMA] * 2
         + [pltpu.SemaphoreType.DMA((7,)), pltpu.SemaphoreType.DMA((7,))],
         compiler_params=pltpu.CompilerParams(
-            collective_id=0, has_side_effects=True, vmem_limit_bytes=60 * 1024 * 1024
+            collective_id=0, has_side_effects=True, vmem_limit_bytes=61 * 1024 * 1024
         ),
     )(*operands)
+    return pl.pallas_call(
+        store_kernel,
+        out_shape=results,
+        in_specs=[pl.BlockSpec(memory_space=pl.ANY)] * 4,
+        out_specs=(pl.BlockSpec(memory_space=pl.ANY),) * 4,
+        scratch_shapes=[pltpu.VMEM(x.shape, x.dtype) for x in results]
+        + [pltpu.SemaphoreType.DMA((4,))] * 2,
+        compiler_params=pltpu.CompilerParams(
+            has_side_effects=True, vmem_limit_bytes=61 * 1024 * 1024
+        ),
+    )(*outs)
 
 
 def solution(mesh):

time: 56.9 us -> 51.2 us (0.90)
  local copies, waits for them, and re-layouts: 3.94 us -> 0 us
  Pallas kernels: 52.1 us -> 50.4 us
    unnamed x10 -> x0, local copies, waits for them, and re-layouts: 3.94 us -> none
    pallas_call x1, Pallas kernels: 52.1 us -> 48.3 us  [shards(): pl.pallas_call(kernel, out_shape=results, in_specs=[pl.BlockSpec(memory_s...]
    pallas_call x0 -> x1, Pallas kernels: none -> 2.14 us  [shards(): pl.pallas_call(store_kernel, out_shape=results, in_specs=[pl.BlockSpec(me...]
where the time goes in v3:
time: 51.2 us; the launch traced here: 51.1 us
  Pallas kernels  50.4 us (98%)
  between operations  0.64 us (1%)
    pallas_call x1, Pallas kernels, shards(): pl.pallas_call(kernel, out_shape=results, in_specs=[pl.BlockSpec(memory_s...  48.3 us
    pallas_call x1, Pallas kernels, shards(): pl.pallas_call(store_kernel, out_shape=results, in_specs=[pl.BlockSpec(me...  2.14 us

profile of v3, /device:TPU:1, one launch (start us, length us, event | category | flops | bytes accessed | tf_op | source)
XLA Modules:
  0.0 51.1 jit_solution(7894892734679745389)
XLA Ops:
  0.6 48.3 %shard_map.102 = (bf16[1,512,256]{2,1,0:T(8,128)(2,1)}, bf16[1,512,256]{2,1,0:T(8,128)(2,1)}, bf16[1,512,256]{2,1,0:T(8,128)(2,1)}, f32[512,256]{1,0:T(8,128)}) custom-call(bf16[1,512,256]{2,1,0:T(8,128)(2,1)} %query_in.1, bf16[1,512,256]{2,1,0:T(8,128)(2,1)} %key_hbm.1, bf16[1,512,256]{2,1,0:T(8,128)(2,1)} %value_in.1, bf16[1,512,256]{2,1,0:T(8,128)(2,1)} %grad_in.1, ...), custom_call_target="tpu_custom_call" | custom-call | tf_op jit(solution)/shard_map/pallas_call | solution.py:430
  48.9 2.1 %shard_map.103 = (bf16[1,512,256]{2,1,0:T(8,128)(2,1)}, bf16[1,512,256]{2,1,0:T(8,128)(2,1)}, bf16[1,512,256]{2,1,0:T(8,128)(2,1)}, f32[512,256]{1,0:T(8,128)}) custom-call(bf16[1,512,256]{2,1,0:T(8,128)(2,1)} %get-tuple-element.8.refs_0_, bf16[1,512,256]{2,1,0:T(8,128)(2,1)} %get-tuple-element.9.refs_1_, bf16[1,512,256]{2,1,0:T(8,128)(2,1)} %get-tuple-element.10.refs_2_, ...), custom_call_target="tpu_custom_call" | custom-call | tf_op jit(solution)/shard_map/pallas_call | solution.py:447

commit v4 on v3

--- a/solution.py
+++ b/solution.py
@@ -67,15 +67,13 @@
     s_gd, r_gd, s_taps, r_taps, s_ret, r_ret,
     f_gd, f_taps, c_part, z_part, z_sum, z_all,
     x_send, x_recv, m_send, m_recv, rs_send, rs_recv, ag_send, ag_recv,
-    pair_send, pair_recv, load_sem, store_sem,
+    load_sem, store_sem,
 ):
     dp = lax.axis_index("dp")
     me = lax.axis_index("seq")
     tp = lax.axis_index("tp")
     chip, core = me // 2, lax.rem(me, 2)
     x_at, y_at = chip // 4, lax.rem(chip, 4)
-    odd = lax.rem(dp, 2)
-    mate = dp + 1 - 2 * odd
 
     loads = [
         pltpu.make_async_copy(src, dst, load_sem.at[i])
@@ -131,7 +129,7 @@
         pltpu.make_async_copy(src.at[mine], dst.at[mine], x_recv.at[index]).start()
 
     def arrived(index, dst, base):
-        part = dst.at[pl.ds(pl.multiple_of(base, 512), 512)]
+        part = dst.at[pl.ds(base, 512)]
         pltpu.make_async_copy(part, part, x_recv.at[index]).wait()
 
 
@@ -152,18 +150,14 @@
                         pl.ds(at + c, 32, stride=2), :
                     ]
 
-    def pack_taps():
-        for h in range(2):
-            for a in range(4):
-                at = (h * 4 + a) * LANES
-                t_taps[pl.ds(at, LANES), :] = taps[pl.ds(LANES * a, LANES), pl.ds(LANES * h, LANES)].T
-        for h in range(2):
-            for a in range(4):
-                at = (h * 4 + a) * LANES
-                for c in range(2):
-                    s_taps[pl.ds(a * 4 + h * 2 + c, 32, stride=16), :] = t_taps[
-                        pl.ds(at + 64 * odd + c, 32, stride=2), :
-                    ]
+    def pack_taps(h):
+        for a in range(4):
+            at = (h * 4 + a) * LANES
+            t_taps[pl.ds(at, LANES), :] = taps[pl.ds(LANES * a, LANES), pl.ds(LANES * h, LANES)].T
+            for v in range(4):
+                s_taps[pl.ds(h * 512 + a * 4 + v, 32, stride=16), :] = t_taps[
+                    pl.ds(at + 64 * (v // 2) + v % 2, 32, stride=2), :
+                ]
 
 
     def forward(src, base):
@@ -195,7 +189,7 @@
         return dot(last_h[...], zh) + dot(last_h[...], zl) + dot(last_l[...], zh)
 
     def spec_at(p, sig):
-        return pl.ds(pl.multiple_of((p * 2 + sig) * 256, 256), 256)
+        return pl.ds((p * 2 + sig) * 256, 256)
 
     def gate_chunk(p):
         gate = forward(r_gd, p * 512)
@@ -257,15 +251,11 @@
                 device_id_type=MESH,
             ).start()
 
-    def forward_taps(half):
-        base = pl.multiple_of(half * 512, 512)
-        for h in range(2):
-            f_taps[pl.ds(pl.multiple_of((2 * h + half) * 256, 256), 256), :] = forward(
-                r_taps, base + 2 * h
-            )
+    def forward_taps(p):
+        f_taps[pl.ds(p * 256, 256), :] = forward(r_taps, (p // 2) * 512 + 2 * (p % 2))
 
     def return_chunk(p):
-        filt = f_taps[pl.ds(pl.multiple_of(p * 256, 256), 256), :]
+        filt = f_taps[pl.ds(p * 256, 256), :]
         conv = inverse(filt, f_gd[spec_at(p, 0), :], False)
         adj = inverse(filt, f_gd[spec_at(p, 1), :], True)
         for v in range(4):
@@ -273,17 +263,33 @@
             s_ret[pl.ds(p * 512 + v, LANES, stride=4), :] = y[:, LANES * (v % 2) : LANES * (v % 2 + 1)]
 
     def send_chunk(p):
-        exchange(5 + p, s_ret, r_ret, p * 512)
-
-    def unpack_chunk(h, part):
-        p = 2 * h + part
-        arrived(5 + p, r_ret, p * 512)
+        exchange(6 + p, s_ret, r_ret, p * 512)
+
+    def unpack_chunk(p):
+        arrived(6 + p, r_ret, p * 512)
         for sig in range(2):
             for a in range(4):
+                at = (((p // 2) * 2 + sig) * 4 + a) * LANES + 64 * (p % 2)
                 for c in range(2):
-                    t_ret[
-                        pl.ds(((h * 2 + sig) * 4 + a) * LANES + 64 * part + c, 32, stride=2), :
-                    ] = r_ret[pl.ds(p * 512 + a * 4 + sig * 2 + c, 32, stride=16), :]
+                    t_ret[pl.ds(at + c, 32, stride=2), :] = r_ret[
+                        pl.ds(p * 512 + a * 4 + sig * 2 + c, 32, stride=16), :
+                    ]
+
+    def unpack_filter(p):
+        part = z_all.at[pl.ds(0, DP - 1), :, pl.ds(2 * p, 2)]
+        pltpu.make_async_copy(part, part, ag_recv.at[p]).wait()
+        for a in range(4):
+            at = ((p // 2) * 4 + a) * LANES + 64 * (p % 2)
+            for c in range(2):
+                t_filt[pl.ds(at + c, 32, stride=2), :] = z_all[a, :, 2 * p + c, :]
+
+    def finish_filter(h):
+        c = pl.ds(LANES * h, LANES)
+        for a in range(4):
+            o_filter[pl.ds(LANES * a, LANES), c] = t_filt[pl.ds((h * 4 + a) * LANES, LANES), :].T
+        store = pltpu.make_async_copy(o_filter.at[:, c], out_filter.at[:, c], store_sem.at[6 + h])
+        store.start()
+        stores.append(store)
 
     def finish(h):
         c = pl.ds(LANES * h, LANES)
@@ -302,8 +308,6 @@
             stores.append(store)
 
     stores = []
-    own_taps = r_taps.at[pl.ds(pl.multiple_of(odd * 512, 512), 512)]
-    other_taps = r_taps.at[pl.ds(pl.multiple_of((1 - odd) * 512, 512), 512)]
     loads[0].wait()
     loads[1].wait()
     loads[2].wait()
@@ -312,82 +316,64 @@
     pack_gd(0)
     pl.semaphore_wait(barrier, SEQ + DP - 2)
     exchange(0, s_gd, r_gd, 0)
-    loads[4].wait()
-    pack_taps()
-    exchange(4, s_taps, own_taps, 0)
     pack_gd(1)
     exchange(1, s_gd, r_gd, 512)
+    loads[4].wait()
+    pack_taps(0)
+    exchange(4, s_taps, r_taps, 0)
     transpose_gd(1)
     pack_gd(2)
     exchange(2, s_gd, r_gd, 1024)
     pack_gd(3)
-    exchange(3, s_gd, r_gd, 1536)
     loads[5].wait()
     loads[6].wait()
     arrived(0, r_gd, 0)
     gate_chunk(0)
-    arrived(4, own_taps, 0)
-    pair = pltpu.make_async_remote_copy(
-        src_ref=own_taps,
-        dst_ref=own_taps,
-        send_sem=pair_send,
-        recv_sem=pair_recv,
-        device_id=(mate, me, tp),
-        device_id_type=MESH,
-    )
-    pair.start()
-    forward_taps(odd)
     arrived(1, r_gd, 512)
     gate_chunk(1)
-    return_chunk(odd)
-    send_chunk(odd)
     sum_chunk(0)
+    exchange(3, s_gd, r_gd, 1536)
+    pack_taps(1)
+    exchange(5, s_taps, r_taps, 512)
+    arrived(4, r_taps, 0)
+    forward_taps(0)
+    forward_taps(1)
+    return_chunk(0)
+    send_chunk(0)
     arrived(2, r_gd, 1024)
     gate_chunk(2)
-    pltpu.make_async_copy(other_taps, other_taps, pair_recv).wait()
-    forward_taps(1 - odd)
-    return_chunk(1 - odd)
-    send_chunk(1 - odd)
     sum_chunk(1)
     spread_chunk(0)
+    return_chunk(1)
+    send_chunk(1)
     arrived(3, r_gd, 1536)
     gate_chunk(3)
-    return_chunk(2 + odd)
-    send_chunk(2 + odd)
     sum_chunk(2)
+    arrived(5, r_taps, 512)
+    forward_taps(2)
+    return_chunk(2)
     spread_chunk(1)
-    return_chunk(3 - odd)
+    forward_taps(3)
     sum_chunk(3)
-    send_chunk(3 - odd)
+    send_chunk(2)
+    return_chunk(3)
+    send_chunk(3)
+    unpack_chunk(0)
+    unpack_chunk(1)
+    finish(0)
     spread_chunk(2)
-    unpack_chunk(0, odd)
-    unpack_chunk(0, 1 - odd)
-    finish(0)
+    unpack_filter(0)
     spread_chunk(3)
-    unpack_chunk(1, odd)
-    unpack_chunk(1, 1 - odd)
+    unpack_filter(1)
+    finish_filter(0)
+    unpack_chunk(2)
+    unpack_chunk(3)
     finish(1)
-
-    for p in range(4):
-        part = z_all.at[pl.ds(0, DP - 1), :, pl.ds(2 * p, 2)]
-        pltpu.make_async_copy(part, part, ag_recv.at[p]).wait()
-        for a in range(4):
-            for c in range(2):
-                t_filt[
-                    pl.ds(((p // 2) * 4 + a) * LANES + 64 * (p % 2) + c, 32, stride=2), :
-                ] = z_all[a, :, 2 * p + c, :]
-    for h in range(2):
-        for a in range(4):
-            o_filter[pl.ds(LANES * a, LANES), pl.ds(LANES * h, LANES)] = t_filt[
-                pl.ds((h * 4 + a) * LANES, LANES), :
-            ].T
-
-    store = pltpu.make_async_copy(o_filter, out_filter, store_sem.at[6])
-    store.start()
-    stores.append(store)
-
-    pair.wait_send()
-    for index in range(9):
+    unpack_filter(2)
+    unpack_filter(3)
+    finish_filter(1)
+
+    for index in range(10):
         part = s_gd.at[pl.ds(0, 496)]
         pltpu.make_async_copy(part, part, x_send.at[index]).wait()
     for p in range(4):
@@ -434,12 +420,11 @@
         out_specs=(pl.BlockSpec(memory_space=pl.ANY),) * 4,
         scratch_shapes=[pltpu.VMEM(x.shape, x.dtype) for x in operands + results]
         + [block(2048), block(1024), block(1024), block(2048), block(1024)]
-        + [block(2048), block(2048), block(512), block(1024), block(2048), block(2048)]
+        + [block(2048), block(2048), block(1024), block(1024), block(2048), block(2048)]
         + [block(2048, 2 * LANES), block(1024, 2 * LANES), block(1024), block(768)]
         + [pltpu.VMEM((SEQ, 8, LANES), F32), pltpu.VMEM((DP, SEQ, 8, LANES), F32)]
-        + [pltpu.SemaphoreType.DMA((n,)) for n in (9, 9, 4, 4, 4, 4, 4, 4)]
-        + [pltpu.SemaphoreType.DMA] * 2
-        + [pltpu.SemaphoreType.DMA((7,)), pltpu.SemaphoreType.DMA((7,))],
+        + [pltpu.SemaphoreType.DMA((n,)) for n in (10, 10, 4, 4, 4, 4, 4, 4)]
+        + [pltpu.SemaphoreType.DMA((7,)), pltpu.SemaphoreType.DMA((8,))],
         compiler_params=pltpu.CompilerParams(
             collective_id=0, has_side_effects=True, vmem_limit_bytes=61 * 1024 * 1024
         ),

time: 51.2 us -> 47.9 us (0.936)
  Pallas kernels: 50.4 us -> 47.1 us
    pallas_call x1, Pallas kernels: 48.3 us -> 45 us  [shards(): pl.pallas_call(kernel, out_shape=results, in_specs=[pl.BlockSpec(memory_s...]
where the time goes in v4:
time: 47.9 us; the launch traced here: 47.8 us
  Pallas kernels  47.1 us (98%)
  between operations  0.64 us (1%)
    pallas_call x1, Pallas kernels, shards(): pl.pallas_call(kernel, out_shape=results, in_specs=[pl.BlockSpec(memory_s...  45 us
    pallas_call x1, Pallas kernels, shards(): pl.pallas_call(store_kernel, out_shape=results, in_specs=[pl.BlockSpec(me...  2.14 us

profile of v4, /device:TPU:1, one launch (start us, length us, event | category | flops | bytes accessed | tf_op | source)
XLA Modules:
  0.0 47.8 jit_solution(9822380081829215296)
XLA Ops:
  0.6 45.0 %shard_map.102 = (bf16[1,512,256]{2,1,0:T(8,128)(2,1)}, bf16[1,512,256]{2,1,0:T(8,128)(2,1)}, bf16[1,512,256]{2,1,0:T(8,128)(2,1)}, f32[512,256]{1,0:T(8,128)}) custom-call(bf16[1,512,256]{2,1,0:T(8,128)(2,1)} %query_in.1, bf16[1,512,256]{2,1,0:T(8,128)(2,1)} %key_hbm.1, bf16[1,512,256]{2,1,0:T(8,128)(2,1)} %value_in.1, bf16[1,512,256]{2,1,0:T(8,128)(2,1)} %grad_in.1, ...), custom_call_target="tpu_custom_call" | custom-call | tf_op jit(solution)/shard_map/pallas_call | solution.py:416
  45.6 2.1 %shard_map.103 = (bf16[1,512,256]{2,1,0:T(8,128)(2,1)}, bf16[1,512,256]{2,1,0:T(8,128)(2,1)}, bf16[1,512,256]{2,1,0:T(8,128)(2,1)}, f32[512,256]{1,0:T(8,128)}) custom-call(bf16[1,512,256]{2,1,0:T(8,128)(2,1)} %get-tuple-element.8.refs_0_, bf16[1,512,256]{2,1,0:T(8,128)(2,1)} %get-tuple-element.9.refs_1_, bf16[1,512,256]{2,1,0:T(8,128)(2,1)} %get-tuple-element.10.refs_2_, ...), custom_call_target="tpu_custom_call" | custom-call | tf_op jit(solution)/shard_map/pallas_call | solution.py:432

commit v5 on v4

--- a/solution.py
+++ b/solution.py
@@ -223,23 +223,22 @@
             total = c_part[pl.ds(p * 256 + dp * 64 + c, 32, stride=2), :]
             for step in range(DP - 1):
                 total = total + z_part[pl.ds((p * 3 + step) * 64 + c, 32, stride=2), :]
-            z_sum[:, 2 * p + c, :] = total * scale
-        two = pl.ds(2 * p, 2)
+            z_sum[p, :, c, :] = total * scale
 
         for to in partners:
             pltpu.make_async_remote_copy(
-                src_ref=z_sum.at[to, two],
-                dst_ref=z_all.at[dp, me, two],
+                src_ref=z_sum.at[p, to],
+                dst_ref=z_all.at[dp, p, me],
                 send_sem=m_send.at[p],
                 recv_sem=m_recv.at[p],
                 device_id=(dp, to, tp),
                 device_id_type=MESH,
             ).start()
 
-        pltpu.make_async_copy(z_sum.at[me, two], z_all.at[dp, me, two], m_recv.at[p]).start()
+        pltpu.make_async_copy(z_sum.at[p, me], z_all.at[dp, p, me], m_recv.at[p]).start()
 
     def spread_chunk(p):
-        part = z_all.at[dp, :, pl.ds(2 * p, 2)]
+        part = z_all.at[dp, p]
         pltpu.make_async_copy(part, part, m_recv.at[p]).wait()
         for step in range(1, DP):
             pltpu.make_async_remote_copy(
@@ -276,12 +275,12 @@
                     ]
 
     def unpack_filter(p):
-        part = z_all.at[pl.ds(0, DP - 1), :, pl.ds(2 * p, 2)]
+        part = z_all.at[pl.ds(0, DP - 1), p]
         pltpu.make_async_copy(part, part, ag_recv.at[p]).wait()
         for a in range(4):
             at = ((p // 2) * 4 + a) * LANES + 64 * (p % 2)
             for c in range(2):
-                t_filt[pl.ds(at + c, 32, stride=2), :] = z_all[a, :, 2 * p + c, :]
+                t_filt[pl.ds(at + c, 32, stride=2), :] = z_all[a, p, :, c, :]
 
     def finish_filter(h):
         c = pl.ds(LANES * h, LANES)
@@ -377,11 +376,11 @@
         part = s_gd.at[pl.ds(0, 496)]
         pltpu.make_async_copy(part, part, x_send.at[index]).wait()
     for p in range(4):
-        part = z_sum.at[pl.ds(0, SEQ - 1), pl.ds(0, 2)]
+        part = z_sum.at[0, pl.ds(0, SEQ - 1)]
         pltpu.make_async_copy(part, part, m_send.at[p]).wait()
         part = z_part.at[pl.ds(0, 192)]
         pltpu.make_async_copy(part, part, rs_send.at[p]).wait()
-        part = z_all.at[pl.ds(0, DP - 1), :, pl.ds(0, 2)]
+        part = z_all.at[pl.ds(0, DP - 1), 0]
         pltpu.make_async_copy(part, part, ag_send.at[p]).wait()
     for store in stores:
         store.wait()
@@ -422,7 +421,7 @@
         + [block(2048), block(1024), block(1024), block(2048), block(1024)]
         + [block(2048), block(2048), block(1024), block(1024), block(2048), block(2048)]
         + [block(2048, 2 * LANES), block(1024, 2 * LANES), block(1024), block(768)]
-        + [pltpu.VMEM((SEQ, 8, LANES), F32), pltpu.VMEM((DP, SEQ, 8, LANES), F32)]
+        + [pltpu.VMEM((4, SEQ, 2, LANES), F32), pltpu.VMEM((DP, 4, SEQ, 2, LANES), F32)]
         + [pltpu.SemaphoreType.DMA((n,)) for n in (10, 10, 4, 4, 4, 4, 4, 4)]
         + [pltpu.SemaphoreType.DMA((7,)), pltpu.SemaphoreType.DMA((8,))],
         compiler_params=pltpu.CompilerParams(

time: 47.9 us -> 47.9 us (level)
  no operation moved by 1% of the time
where the time goes in v5:
time: 47.9 us; the launch traced here: 47.8 us
  Pallas kernels  47.1 us (98%)
  between operations  0.64 us (1%)
    pallas_call x1, Pallas kernels, shards(): pl.pallas_call(kernel, out_shape=results, in_specs=[pl.BlockSpec(memory_s...  45 us
    pallas_call x1, Pallas kernels, shards(): pl.pallas_call(store_kernel, out_shape=results, in_specs=[pl.BlockSpec(me...  2.14 us

profile of v5, /device:TPU:1, one launch (start us, length us, event | category | flops | bytes accessed | tf_op | source)
XLA Modules:
  0.0 47.8 jit_solution(6152603056158772787)
XLA Ops:
  0.6 45.0 %shard_map.102 = (bf16[1,512,256]{2,1,0:T(8,128)(2,1)}, bf16[1,512,256]{2,1,0:T(8,128)(2,1)}, bf16[1,512,256]{2,1,0:T(8,128)(2,1)}, f32[512,256]{1,0:T(8,128)}) custom-call(bf16[1,512,256]{2,1,0:T(8,128)(2,1)} %query_in.1, bf16[1,512,256]{2,1,0:T(8,128)(2,1)} %key_hbm.1, bf16[1,512,256]{2,1,0:T(8,128)(2,1)} %value_in.1, bf16[1,512,256]{2,1,0:T(8,128)(2,1)} %grad_in.1, ...), custom_call_target="tpu_custom_call" | custom-call | tf_op jit(solution)/shard_map/pallas_call | solution.py:415
  45.6 2.1 %shard_map.103 = (bf16[1,512,256]{2,1,0:T(8,128)(2,1)}, bf16[1,512,256]{2,1,0:T(8,128)(2,1)}, bf16[1,512,256]{2,1,0:T(8,128)(2,1)}, f32[512,256]{1,0:T(8,128)}) custom-call(bf16[1,512,256]{2,1,0:T(8,128)(2,1)} %get-tuple-element.8.refs_0_, bf16[1,512,256]{2,1,0:T(8,128)(2,1)} %get-tuple-element.9.refs_1_, bf16[1,512,256]{2,1,0:T(8,128)(2,1)} %get-tuple-element.10.refs_2_, ...), custom_call_target="tpu_custom_call" | custom-call | tf_op jit(solution)/shard_map/pallas_call | solution.py:431

commit v6 on v4

--- a/solution.py
+++ b/solution.py
@@ -75,21 +75,15 @@
     chip, core = me // 2, lax.rem(me, 2)
     x_at, y_at = chip // 4, lax.rem(chip, 4)
 
+    moves = [
+        (src.at[:, :, pl.ds(LANES * h, LANES)], dst.at[:, :, pl.ds(LANES * h, LANES)])
+        for h in range(2)
+        for src, dst in ((key_hbm, key_in), (value_in, value), (grad_in, grad), (query_in, query))
+    ] + [(taps_in, taps), (mats_in, mats), (turns_in, turns)]
     loads = [
-        pltpu.make_async_copy(src, dst, load_sem.at[i])
-        for i, (src, dst) in enumerate(
-            (
-                (key_hbm, key_in),
-                (value_in, value),
-                (grad_in, grad),
-                (query_in, query),
-                (taps_in, taps),
-                (mats_in, mats),
-                (turns_in, turns),
-            )
-        )
+        pltpu.make_async_copy(src, dst, load_sem.at[i]) for i, (src, dst) in enumerate(moves)
     ]
-    for load in loads:
+    for load in loads[:4]:
         load.start()
     first_cat = mats.at[pl.ds(0, 256)]
     first_l = mats.at[pl.ds(256, 256), pl.ds(0, LANES)]
@@ -287,9 +281,12 @@
         c = pl.ds(LANES * h, LANES)
         for a in range(4):
             o_filter[pl.ds(LANES * a, LANES), c] = t_filt[pl.ds((h * 4 + a) * LANES, LANES), :].T
-        store = pltpu.make_async_copy(o_filter.at[:, c], out_filter.at[:, c], store_sem.at[6 + h])
-        store.start()
-        stores.append(store)
+        store(o_filter.at[:, c], out_filter.at[:, c])
+
+    def store(src, dst):
+        copy = pltpu.make_async_copy(src, dst, store_sem.at[len(stores)])
+        copy.start()
+        stores.append(copy)
 
     def finish(h):
         c = pl.ds(LANES * h, LANES)
@@ -300,33 +297,34 @@
             o_query[0, p, c] = (grad[0, p, c].astype(F32) * conv).astype(BF)
             o_key[0, p, c] = (adj * value[0, p, c].astype(F32)).astype(BF)
             o_value[0, p, c] = (adj * key_in[0, p, c].astype(F32)).astype(BF)
-        for i, (src, dst) in enumerate(
-            ((o_query, out_query), (o_key, out_key), (o_value, out_value))
-        ):
-            store = pltpu.make_async_copy(src.at[:, :, c], dst.at[:, :, c], store_sem.at[2 * i + h])
-            store.start()
-            stores.append(store)
+            if a % 2 == 1:
+                two = pl.ds(LANES * (a - 1), 2 * LANES)
+                store(o_query.at[:, two, c], out_query.at[:, two, c])
+                store(o_key.at[:, two, c], out_key.at[:, two, c])
+                store(o_value.at[:, two, c], out_value.at[:, two, c])
 
     stores = []
-    loads[0].wait()
-    loads[1].wait()
-    loads[2].wait()
-    loads[3].wait()
+    for load in loads[:4]:
+        load.wait()
+    for load in loads[4:]:
+        load.start()
     transpose_gd(0)
     pack_gd(0)
     pl.semaphore_wait(barrier, SEQ + DP - 2)
     exchange(0, s_gd, r_gd, 0)
     pack_gd(1)
     exchange(1, s_gd, r_gd, 512)
-    loads[4].wait()
+    loads[8].wait()
     pack_taps(0)
     exchange(4, s_taps, r_taps, 0)
+    for load in loads[4:8]:
+        load.wait()
     transpose_gd(1)
     pack_gd(2)
     exchange(2, s_gd, r_gd, 1024)
     pack_gd(3)
-    loads[5].wait()
-    loads[6].wait()
+    loads[9].wait()
+    loads[10].wait()
     arrived(0, r_gd, 0)
     gate_chunk(0)
     arrived(1, r_gd, 512)
@@ -383,8 +381,8 @@
         pltpu.make_async_copy(part, part, rs_send.at[p]).wait()
         part = z_all.at[pl.ds(0, DP - 1), :, pl.ds(0, 2)]
         pltpu.make_async_copy(part, part, ag_send.at[p]).wait()
-    for store in stores:
-        store.wait()
+    for copy in stores:
+        copy.wait()
 
 
 def store_kernel(*refs):
@@ -424,7 +422,7 @@
         + [block(2048, 2 * LANES), block(1024, 2 * LANES), block(1024), block(768)]
         + [pltpu.VMEM((SEQ, 8, LANES), F32), pltpu.VMEM((DP, SEQ, 8, LANES), F32)]
         + [pltpu.SemaphoreType.DMA((n,)) for n in (10, 10, 4, 4, 4, 4, 4, 4)]
-        + [pltpu.SemaphoreType.DMA((7,)), pltpu.SemaphoreType.DMA((8,))],
+        + [pltpu.SemaphoreType.DMA((11,)), pltpu.SemaphoreType.DMA((14,))],
         compiler_params=pltpu.CompilerParams(
             collective_id=0, has_side_effects=True, vmem_limit_bytes=61 * 1024 * 1024
         ),

time: 47.9 us -> 48 us (level)
  no operation moved by 1% of the time
where the time goes in v6:
time: 48 us; the launch traced here: 47.9 us
  Pallas kernels  47.2 us (98%)
  between operations  0.64 us (1%)
    pallas_call x1, Pallas kernels, shards(): pl.pallas_call(kernel, out_shape=results, in_specs=[pl.BlockSpec(memory_s...  45.1 us
    pallas_call x1, Pallas kernels, shards(): pl.pallas_call(store_kernel, out_shape=results, in_specs=[pl.BlockSpec(me...  2.14 us

profile of v6, /device:TPU:1, one launch (start us, length us, event | category | flops | bytes accessed | tf_op | source)
XLA Modules:
  0.0 47.9 jit_solution(6869711334129432098)
XLA Ops:
  0.6 45.1 %shard_map.102 = (bf16[1,512,256]{2,1,0:T(8,128)(2,1)}, bf16[1,512,256]{2,1,0:T(8,128)(2,1)}, bf16[1,512,256]{2,1,0:T(8,128)(2,1)}, f32[512,256]{1,0:T(8,128)}) custom-call(bf16[1,512,256]{2,1,0:T(8,128)(2,1)} %query_in.1, bf16[1,512,256]{2,1,0:T(8,128)(2,1)} %key_hbm.1, bf16[1,512,256]{2,1,0:T(8,128)(2,1)} %value_in.1, bf16[1,512,256]{2,1,0:T(8,128)(2,1)} %grad_in.1, ...), custom_call_target="tpu_custom_call" | custom-call | tf_op jit(solution)/shard_map/pallas_call | solution.py:414
  45.7 2.1 %shard_map.103 = (bf16[1,512,256]{2,1,0:T(8,128)(2,1)}, bf16[1,512,256]{2,1,0:T(8,128)(2,1)}, bf16[1,512,256]{2,1,0:T(8,128)(2,1)}, f32[512,256]{1,0:T(8,128)}) custom-call(bf16[1,512,256]{2,1,0:T(8,128)(2,1)} %get-tuple-element.8.refs_0_, bf16[1,512,256]{2,1,0:T(8,128)(2,1)} %get-tuple-element.9.refs_1_, bf16[1,512,256]{2,1,0:T(8,128)(2,1)} %get-tuple-element.10.refs_2_, ...), custom_call_target="tpu_custom_call" | custom-call | tf_op jit(solution)/shard_map/pallas_call | solution.py:430
